TPU v7x, 128 devices: a whole 4x4x4 slice. The times are simulated.
128 devices in a mesh: slab: 16 (over z, x_hi, core), view: 8 (over x_lo, y).
Axes of the slice: x: 4 (x_hi: 2, x_lo: 2; x = x_hi * 2 + x_lo), y: 4, z: 4, core: 2. Of those that a mesh axis runs over, the one named last changes fastest.
Arguments:
- estimate: float32 [512, 128, 256], P('slab'), may hold values from 0.5 to 2
- views_data: float32 [8, 512, 128, 256], P('view', 'slab'), may hold values from 0.2 to 5
- counts: int32 [8, 512, 128], P(None, 'slab'), may hold values from 1 to 4
- psf: float32 [8, 3, 31], P('view'), may hold values from 0.05 to 1
Outputs:
- deconvolved: float32 [512, 128, 256], P('slab')
All inputs are finite; a program needn't handle non-finite values.
Results may differ from a plain program's by a relative error of at most 0.00007.
Values sent between devices are 32-bit elements; how exact they have to be, the bound alone decides.
A program may use at most 128 MiB of HBM per device.

v0:
```python
import jax
import jax.numpy as jnp
from jax import lax
from jax.sharding import PartitionSpec as P

ITERS = 2


def padded_2(value, sides, width):
    for axis, dim in sides:
        peers, length = (lax.axis_size(axis), value.shape[dim])
        up = [(i, (i + 1) % peers) for i in range(peers - 1)]
        down = [(j, i) for i, j in up]
        last = lax.slice_in_dim(value, length - width, length, axis=dim)
        initial = lax.slice_in_dim(value, 0, width, axis=dim)
        before = lax.ppermute(last, axis, up)
        after = lax.ppermute(initial, axis, down)
        value = jnp.concatenate([before, value, after], axis=dim)
    return value


def band_matrix(kernel, rows, columns, orient, offset):
    taps_count = kernel.shape[0]
    out_index = lax.broadcasted_iota(jnp.int32, (rows, columns), 0)
    in_index = lax.broadcasted_iota(jnp.int32, (rows, columns), 1)
    distance = orient * (out_index - in_index) + offset
    values = jnp.zeros((rows, columns), jnp.float32)
    for tap_index in range(taps_count):
        values = values + jnp.where(distance == tap_index, kernel[tap_index], jnp.float32(0.0))
    return values


def convolve(padded, z_matrix, y_matrix, x_matrix):
    highest = lax.Precision.HIGHEST
    volume = jnp.einsum("wz,zyx->wyx", z_matrix, padded, precision=highest)
    volume = jnp.einsum("vy,zyx->zvx", y_matrix, volume, precision=highest)
    return jnp.einsum("wx,zyx->zyw", x_matrix, volume, precision=highest)


def shards(estimate, views_data, counts, psf):
    kernel = psf[0] / jnp.sum(psf[0], axis=1, keepdims=True)
    half_width = (psf.shape[2] - 1) // 2
    depth, height, breadth = estimate.shape
    recording = views_data[0]
    counts_float = counts.astype(jnp.float32)
    total_counts = jnp.sum(counts_float, axis=0)
    own_counts = lax.dynamic_index_in_dim(counts_float, lax.axis_index("view"), 0, keepdims=False)
    weight = (own_counts / total_counts)[:, :, None]
    y_blur = band_matrix(kernel[1], height, height, 1, half_width)
    y_back = band_matrix(kernel[1], height, height, -1, half_width)
    x_blur = band_matrix(kernel[2], breadth, breadth, 1, half_width)
    x_back = band_matrix(kernel[2], breadth, breadth, -1, half_width)
    z_back = band_matrix(kernel[0], depth, depth + 2 * half_width, -1, 0)
    z_blur = band_matrix(kernel[0], depth, depth + 2 * half_width, 1, 2 * half_width)
    current = estimate
    for step in range(ITERS):
        padded = padded_2(current, (("slab", 0),), half_width)
        blurred = convolve(padded, z_blur, y_blur, x_blur)
        quotient = recording / blurred
        quotient_padded = padded_2(quotient, (("slab", 0),), half_width)
        back = convolve(quotient_padded, z_back, y_back, x_back)
        update = lax.psum(weight * back, "view")
        current = current * update
    return current


def solution(mesh):
    in_specs = (
        P("slab", None, None),
        P("view", "slab", None, None),
        P(None, "slab", None),
        P("view", None, None),
    )
    out_specs = P("slab", None, None)
    return jax.shard_map(shards, mesh=mesh, in_specs=in_specs, out_specs=out_specs, check_vma=False)
```

profile of v0, /device:TPU:1, one launch (start us, length us, event | category | flops | bytes accessed | tf_op | source)
XLA Modules:
  0.0 762.7 jit_solution(11853196285683659427)
XLA Ops:
  6.5 0.0 copy-start.2
  6.5 0.0 all-reduce.3.cloned.1.call-start
  6.5 3.8 fusion.629
  10.3 6.0 collective-permute-start
  16.4 1.9 collective-permute-start.1
  18.3 0.0 copy-done.2
  18.3 0.1 reduce_sum.19
  18.4 0.1 bitcast_divide_fusion.3
  18.5 0.7 fusion.634
  19.2 0.7 fusion.633
  20.0 0.7 fusion.632
  20.7 0.7 fusion.630
  21.4 0.7 fusion.631
  22.1 16.1 %collective-permute-done = f32[15,128,256]{2,1,0:T(8,128)} collective-permute-done((f32[15,128,256]{2,1,0:T(8,128)}, f32[15,128,256]{2,1,0:T(8,128)}, u32[]{:S(2)}, u32[]{:S(2)}) %collective-permute-start) | collective-permute-done | bytes 1966112 | tf_op jit(solution)/shard_map/ppermute | solution.py:16
  38.2 23.1 %collective-permute-done.1 = f32[15,128,256]{2,1,0:T(8,128)} collective-permute-done((f32[15,128,256]{2,1,0:T(8,128)S(1)}, f32[15,128,256]{2,1,0:T(8,128)}, u32[]{:S(2)}, u32[]{:S(2)}) %collective-permute-start.1) | collective-permute-done | bytes 1966112 | tf_op jit(solution)/shard_map/ppermute | solution.py:17
  61.3 3.8 pad_maximum_fusion
  65.1 28.4 %fusion.6 = f32[32,128,256]{2,0,1:T(8,128)S(1)} fusion(f32[62,128,256]{2,1,0:T(8,128)S(1)} %pad_maximum_fusion, f32[]{:T(128)} %bitcast.31, f32[]{:T(128)} %bitcast.30, f32[]{:T(128)} %bitcast.29, f32[]{:T(128)} %bitcast.28, f32[]{:T(128)} %bitcast.27, f32[]{:T(128)} %bitcast.26, f32[]{:T(128)} %bitcast.25, f32[]{:T(128)} %bitcast.24, f32[]{:T(128)} %bitcast.23, ...), kind=kOutput, calls=%fused_computation.6 | convolution fusion | flops 780327040 | bytes 12320892 | tf_op jit(solution)/shard_map/wz,zyx->wyx/dot_general | solution.py:35
  93.5 0.0 copy-start.3
  93.5 26.5 %fusion.22 = f32[32,256,128]{1,2,0:T(8,128)S(1)} fusion(f32[32,128,256]{2,0,1:T(8,128)S(1)} %fusion.6, f32[]{:T(128)} %bitcast.65, f32[]{:T(128)} %bitcast.64, f32[]{:T(128)} %bitcast.63, f32[]{:T(128)} %bitcast.62, f32[]{:T(128)} %bitcast.61, f32[]{:T(128)} %bitcast.60, f32[]{:T(128)} %bitcast.59, f32[]{:T(128)} %bitcast.58, f32[]{:T(128)} %bitcast.57, ...), kind=kOutput, calls=%fused_computation.28 | convolution fusion | flops 1612152832 | bytes 8388732 | tf_op jit(solution)/shard_map/vy,zyx->zvx/dot_general | solution.py:36
  120.1 0.0 copy-done.3
  120.1 25.2 %bitcast_divide_fusion.1 = f32[32,128,256]{2,1,0:T(8,128)} fusion(f32[1,32,128,256]{3,2,1,0:T(8,128)S(1)} %copy-done.3, f32[32,256,128]{1,2,0:T(8,128)S(1)} %fusion.22, f32[]{:T(128)} %bitcast.98, f32[]{:T(128)} %bitcast.97, f32[]{:T(128)} %bitcast.96, f32[]{:T(128)} %bitcast.95, f32[]{:T(128)} %bitcast.94, f32[]{:T(128)} %bitcast.93, f32[]{:T(128)} %bitcast.92, ...), kind=kOutput, calls=%fused_computation.21 | convolution fusion | flops 3228434432 | bytes 12583036 | tf_op jit(solution)/shard_map/wx,zyx->zyw/dot_general | solution.py:37
  145.3 0.0 copy-start.1
  145.3 3.9 fusion.628
  149.2 1.9 collective-permute-start.2
  151.1 3.7 collective-permute-start.3
  154.8 0.0 copy-done.1
  154.9 18.1 %collective-permute-done.2 = f32[15,128,256]{2,1,0:T(8,128)} collective-permute-done((f32[15,128,256]{2,1,0:T(8,128)}, f32[15,128,256]{2,1,0:T(8,128)}, u32[]{:S(2)}, u32[]{:S(2)}) %collective-permute-start.2) | collective-permute-done | bytes 1966112 | tf_op jit(solution)/shard_map/ppermute | solution.py:16
  173.0 24.2 %collective-permute-done.3 = f32[15,128,256]{2,1,0:T(8,128)} collective-permute-done((f32[15,128,256]{2,1,0:T(8,128)S(1)}, f32[15,128,256]{2,1,0:T(8,128)}, u32[]{:S(2)}, u32[]{:S(2)}) %collective-permute-start.3) | collective-permute-done | bytes 1966112 | tf_op jit(solution)/shard_map/ppermute | solution.py:17
  197.2 4.0 pad_maximum_fusion.1
  201.2 28.4 %fusion.4 = f32[32,128,256]{2,0,1:T(8,128)S(1)} fusion(f32[62,128,256]{2,1,0:T(8,128)S(1)} %pad_maximum_fusion.1, f32[]{:T(128)} %bitcast.31, f32[]{:T(128)} %bitcast.30, f32[]{:T(128)} %bitcast.29, f32[]{:T(128)} %bitcast.28, f32[]{:T(128)} %bitcast.27, f32[]{:T(128)} %bitcast.26, f32[]{:T(128)} %bitcast.25, f32[]{:T(128)} %bitcast.24, f32[]{:T(128)} %bitcast.23, ...), kind=kOutput, calls=%fused_computation.4 | convolution fusion | flops 780327040 | bytes 12320892 | tf_op jit(solution)/shard_map/wz,zyx->wyx/dot_general | solution.py:35
  229.6 26.1 %fusion.20 = f32[32,256,128]{1,2,0:T(8,128)S(1)} fusion(f32[32,128,256]{2,0,1:T(8,128)S(1)} %fusion.4, f32[]{:T(128)} %bitcast.65, f32[]{:T(128)} %bitcast.64, f32[]{:T(128)} %bitcast.63, f32[]{:T(128)} %bitcast.62, f32[]{:T(128)} %bitcast.61, f32[]{:T(128)} %bitcast.60, f32[]{:T(128)} %bitcast.59, f32[]{:T(128)} %bitcast.58, f32[]{:T(128)} %bitcast.57, ...), kind=kOutput, calls=%fused_computation.26 | convolution fusion | flops 1612169216 | bytes 8388732 | tf_op jit(solution)/shard_map/vy,zyx->zvx/dot_general | solution.py:36
  255.7 25.5 %fusion.24 = f32[32,128,256]{2,1,0:T(8,128)} fusion(f32[32,256,128]{1,2,0:T(8,128)S(1)} %fusion.20, f32[32,128]{1,0:T(8,128)S(1)} %bitcast_divide_fusion.2, f32[]{:T(128)} %bitcast.98, f32[]{:T(128)} %bitcast.97, f32[]{:T(128)} %bitcast.96, f32[]{:T(128)} %bitcast.95, f32[]{:T(128)} %bitcast.94, f32[]{:T(128)} %bitcast.93, f32[]{:T(128)} %bitcast.92, ...), kind=kOutput, calls=%fused_computation.30 | convolution fusion | flops 3228499968 | bytes 8405116 | tf_op jit(solution)/shard_map/wx,zyx->zyw/dot_general | solution.py:37
  281.2 0.0 all-reduce.3.cloned.1.call-update
  281.3 0.0 all-reduce.5.cloned.1.call-start
  281.3 104.4 %all-reduce.3.cloned.1.call-done = f32[32,128,256]{2,1,0:T(8,128)} async-done(((f32[32,128,256]{2,1,0:T(8,128)}), f32[32,128,256]{2,1,0:T(8,128)}) %all-reduce.3.cloned.1.call-update) | async-done | bytes 4194320 | tf_op jit(solution)/shard_map/psum | solution.py:62
  385.7 4.1 mul.226
  389.8 0.0 copy-start
  389.8 0.3 fusion.627
  390.0 4.9 collective-permute-start.4
  394.9 1.9 collective-permute-start.5
  396.8 19.6 %collective-permute-done.4 = f32[15,128,256]{2,1,0:T(8,128)S(1)} collective-permute-done((f32[15,128,256]{2,1,0:T(8,128)S(1)}, f32[15,128,256]{2,1,0:T(8,128)S(1)}, u32[]{:S(2)}, u32[]{:S(2)}) %collective-permute-start.4) | collective-permute-done | bytes 1966112 | tf_op jit(solution)/shard_map/ppermute | solution.py:16
  416.5 23.1 %collective-permute-done.5 = f32[15,128,256]{2,1,0:T(8,128)S(1)} collective-permute-done((f32[15,128,256]{2,1,0:T(8,128)S(1)}, f32[15,128,256]{2,1,0:T(8,128)S(1)}, u32[]{:S(2)}, u32[]{:S(2)}) %collective-permute-start.5) | collective-permute-done | bytes 1966112 | tf_op jit(solution)/shard_map/ppermute | solution.py:17
  439.5 1.4 pad_maximum_fusion.2
  440.9 0.0 copy-done
  440.9 28.4 %fusion.2 = f32[32,128,256]{2,0,1:T(8,128)S(1)} fusion(f32[62,128,256]{2,1,0:T(8,128)S(1)} %pad_maximum_fusion.2, f32[]{:T(128)} %bitcast.31, f32[]{:T(128)} %bitcast.30, f32[]{:T(128)} %bitcast.29, f32[]{:T(128)} %bitcast.28, f32[]{:T(128)} %bitcast.27, f32[]{:T(128)} %bitcast.26, f32[]{:T(128)} %bitcast.25, f32[]{:T(128)} %bitcast.24, f32[]{:T(128)} %bitcast.23, ...), kind=kOutput, calls=%fused_computation.2 | convolution fusion | flops 780327040 | bytes 12320892 | tf_op jit(solution)/shard_map/wz,zyx->wyx/dot_general | solution.py:35
  469.3 0.0 copy-start.4
  469.3 26.2 %fusion.18 = f32[32,256,128]{1,2,0:T(8,128)S(1)} fusion(f32[32,128,256]{2,0,1:T(8,128)S(1)} %fusion.2, f32[]{:T(128)} %bitcast.65, f32[]{:T(128)} %bitcast.64, f32[]{:T(128)} %bitcast.63, f32[]{:T(128)} %bitcast.62, f32[]{:T(128)} %bitcast.61, f32[]{:T(128)} %bitcast.60, f32[]{:T(128)} %bitcast.59, f32[]{:T(128)} %bitcast.58, f32[]{:T(128)} %bitcast.57, ...), kind=kOutput, calls=%fused_computation.24 | convolution fusion | flops 1612152832 | bytes 8388732 | tf_op jit(solution)/shard_map/vy,zyx->zvx/dot_general | solution.py:36
  495.6 0.0 copy-done.4
  495.6 23.4 %bitcast_divide_fusion = f32[32,128,256]{2,1,0:T(8,128)S(1)} fusion(f32[1,32,128,256]{3,2,1,0:T(8,128)S(1)} %copy-done.4, f32[32,256,128]{1,2,0:T(8,128)S(1)} %fusion.18, f32[]{:T(128)} %bitcast.98, f32[]{:T(128)} %bitcast.97, f32[]{:T(128)} %bitcast.96, f32[]{:T(128)} %bitcast.95, f32[]{:T(128)} %bitcast.94, f32[]{:T(128)} %bitcast.93, f32[]{:T(128)} %bitcast.92, ...), kind=kOutput, calls=%fused_computation.20 | convolution fusion | flops 3228434432 | bytes 12583036 | tf_op jit(solution)/shard_map/wx,zyx->zyw/dot_general | solution.py:37
  519.0 0.3 fusion.626
  519.2 1.9 collective-permute-start.6
  521.1 2.5 collective-permute-start.7
  523.7 19.0 %collective-permute-done.6 = f32[15,128,256]{2,1,0:T(8,128)S(1)} collective-permute-done((f32[15,128,256]{2,1,0:T(8,128)S(1)}, f32[15,128,256]{2,1,0:T(8,128)S(1)}, u32[]{:S(2)}, u32[]{:S(2)}) %collective-permute-start.6) | collective-permute-done | bytes 1966112 | tf_op jit(solution)/shard_map/ppermute | solution.py:16
  542.7 23.9 %collective-permute-done.7 = f32[15,128,256]{2,1,0:T(8,128)S(1)} collective-permute-done((f32[15,128,256]{2,1,0:T(8,128)S(1)}, f32[15,128,256]{2,1,0:T(8,128)S(1)}, u32[]{:S(2)}, u32[]{:S(2)}) %collective-permute-start.7) | collective-permute-done | bytes 1966112 | tf_op jit(solution)/shard_map/ppermute | solution.py:17
  566.6 1.2 pad_maximum_fusion.3
  567.8 28.4 %fusion = f32[32,128,256]{2,0,1:T(8,128)S(1)} fusion(f32[62,128,256]{2,1,0:T(8,128)S(1)} %pad_maximum_fusion.3, f32[]{:T(128)} %bitcast.31, f32[]{:T(128)} %bitcast.30, f32[]{:T(128)} %bitcast.29, f32[]{:T(128)} %bitcast.28, f32[]{:T(128)} %bitcast.27, f32[]{:T(128)} %bitcast.26, f32[]{:T(128)} %bitcast.25, f32[]{:T(128)} %bitcast.24, f32[]{:T(128)} %bitcast.23, ...), kind=kOutput, calls=%fused_computation | convolution fusion | flops 780327040 | bytes 12320892 | tf_op jit(solution)/shard_map/wz,zyx->wyx/dot_general | solution.py:35
  596.2 26.2 %fusion.16 = f32[32,256,128]{1,2,0:T(8,128)S(1)} fusion(f32[32,128,256]{2,0,1:T(8,128)S(1)} %fusion, f32[]{:T(128)} %bitcast.65, f32[]{:T(128)} %bitcast.64, f32[]{:T(128)} %bitcast.63, f32[]{:T(128)} %bitcast.62, f32[]{:T(128)} %bitcast.61, f32[]{:T(128)} %bitcast.60, f32[]{:T(128)} %bitcast.59, f32[]{:T(128)} %bitcast.58, f32[]{:T(128)} %bitcast.57, ...), kind=kOutput, calls=%fused_computation.22 | convolution fusion | flops 1612169216 | bytes 8388732 | tf_op jit(solution)/shard_map/vy,zyx->zvx/dot_general | solution.py:36
  622.3 25.5 %fusion.27 = f32[32,128,256]{2,1,0:T(8,128)} fusion(f32[32,256,128]{1,2,0:T(8,128)S(1)} %fusion.16, f32[32,128]{1,0:T(8,128)S(1)} %bitcast_divide_fusion.2, f32[]{:T(128)} %bitcast.98, f32[]{:T(128)} %bitcast.97, f32[]{:T(128)} %bitcast.96, f32[]{:T(128)} %bitcast.95, f32[]{:T(128)} %bitcast.94, f32[]{:T(128)} %bitcast.93, f32[]{:T(128)} %bitcast.92, ...), kind=kOutput, calls=%fused_computation.31 | convolution fusion | flops 3228499968 | bytes 8405116 | tf_op jit(solution)/shard_map/wx,zyx->zyw/dot_general | solution.py:37
  647.8 0.0 all-reduce.5.cloned.1.call-update
  647.8 101.4 %all-reduce.5.cloned.1.call-done = f32[32,128,256]{2,1,0:T(8,128)} async-done(((f32[32,128,256]{2,1,0:T(8,128)}), f32[32,128,256]{2,1,0:T(8,128)}) %all-reduce.5.cloned.1.call-update) | async-done | bytes 4194320 | tf_op jit(solution)/shard_map/psum | solution.py:62
  749.2 6.2 mul.228
  (3 shorter events, 0.0 us)
Async XLA Ops:
  6.5 11.8 %copy-start.2 = (f32[1,3,31]{2,0,1:T(1,128)S(1)}, f32[1,3,31]{2,0,1:T(1,128)}, u32[]{:S(2)}) copy-start(f32[1,3,31]{2,0,1:T(1,128)} %param.7) | copy-start | bytes 1120
  6.5 379.1 %all-reduce.3.cloned.1.call-start = ((), (), s32[]{:S(2)}) async-start(), calls=%async_computation | async-start | bytes 8388608 | tf_op jit(solution)/shard_map/psum | solution.py:62
  10.3 27.9 %collective-permute-start = (f32[15,128,256]{2,1,0:T(8,128)}, f32[15,128,256]{2,1,0:T(8,128)}, u32[]{:S(2)}, u32[]{:S(2)}) collective-permute-start(f32[15,128,256]{2,1,0:T(8,128)} %get-tuple-element.11), channel_id=1, source_target_pairs={{0,8},{8,16},{16,24},{24,32},{32,40},{40,48},{48,56},{56,64},{64,7... | collective-permute-start | bytes 5898248 | tf_op jit(solution)/shard_map/ppermute | solution.py:16
  16.4 45.0 %collective-permute-start.1 = (f32[15,128,256]{2,1,0:T(8,128)S(1)}, f32[15,128,256]{2,1,0:T(8,128)}, u32[]{:S(2)}, u32[]{:S(2)}) collective-permute-start(f32[15,128,256]{2,1,0:T(8,128)S(1)} %get-tuple-element.12), channel_id=1, source_target_pairs={{8,0},{16,8},{24,16},{32,24},{40,32},{48,40},{56,48},{64,56},{72,6... | collective-permute-start | bytes 5898248 | tf_op jit(solution)/shard_map/ppermute | solution.py:17
  93.5 26.6 %copy-start.3 = (f32[1,32,128,256]{3,2,1,0:T(8,128)S(1)}, f32[1,32,128,256]{3,2,1,0:T(8,128)}, u32[]{:S(2)}) copy-start(f32[1,32,128,256]{3,2,1,0:T(8,128)} %param.5) | copy-start | bytes 12582916
  145.3 9.5 %copy-start.1 = (s32[8,32,128]{2,1,0:T(8,128)S(1)}, s32[8,32,128]{2,1,0:T(8,128)}, u32[]{:S(2)}) copy-start(s32[8,32,128]{2,1,0:T(8,128)} %param.6) | copy-start | bytes 393220
  149.2 23.8 %collective-permute-start.2 = (f32[15,128,256]{2,1,0:T(8,128)}, f32[15,128,256]{2,1,0:T(8,128)}, u32[]{:S(2)}, u32[]{:S(2)}) collective-permute-start(f32[15,128,256]{2,1,0:T(8,128)} %get-tuple-element.9), channel_id=1, source_target_pairs={{0,8},{8,16},{16,24},{24,32},{32,40},{40,48},{48,56},{56,64},{64,7... | collective-permute-start | bytes 5898248 | tf_op jit(solution)/shard_map/ppermute | solution.py:16
  151.1 46.1 %collective-permute-start.3 = (f32[15,128,256]{2,1,0:T(8,128)S(1)}, f32[15,128,256]{2,1,0:T(8,128)}, u32[]{:S(2)}, u32[]{:S(2)}) collective-permute-start(f32[15,128,256]{2,1,0:T(8,128)S(1)} %get-tuple-element.10), channel_id=1, source_target_pairs={{8,0},{16,8},{24,16},{32,24},{40,32},{48,40},{56,48},{64,56},{72,6... | collective-permute-start | bytes 5898248 | tf_op jit(solution)/shard_map/ppermute | solution.py:17
  281.3 467.9 %all-reduce.5.cloned.1.call-start = ((), (), s32[]{:S(2)}) async-start(), calls=%async_computation.1 | async-start | bytes 8388608 | tf_op jit(solution)/shard_map/psum | solution.py:62
  389.8 51.1 %copy-start = (f32[32,128,256]{2,1,0:T(8,128)}, f32[32,128,256]{2,1,0:T(8,128)S(1)}, u32[]{:S(2)}) copy-start(f32[32,128,256]{2,1,0:T(8,128)S(1)} %mul.226) | copy-start | bytes 12582916
  390.0 26.4 %collective-permute-start.4 = (f32[15,128,256]{2,1,0:T(8,128)S(1)}, f32[15,128,256]{2,1,0:T(8,128)S(1)}, u32[]{:S(2)}, u32[]{:S(2)}) collective-permute-start(f32[15,128,256]{2,1,0:T(8,128)S(1)} %get-tuple-element.7), channel_id=1, source_target_pairs={{0,8},{8,16},{16,24},{24,32},{32,40},{40,48},{48,56},{56,64},{64,7... | collective-permute-start | bytes 5898248 | tf_op jit(solution)/shard_map/ppermute | solution.py:16
  394.9 44.6 %collective-permute-start.5 = (f32[15,128,256]{2,1,0:T(8,128)S(1)}, f32[15,128,256]{2,1,0:T(8,128)S(1)}, u32[]{:S(2)}, u32[]{:S(2)}) collective-permute-start(f32[15,128,256]{2,1,0:T(8,128)S(1)} %get-tuple-element.8), channel_id=1, source_target_pairs={{8,0},{16,8},{24,16},{32,24},{40,32},{48,40},{56,48},{64,56},{72,6... | collective-permute-start | bytes 5898248 | tf_op jit(solution)/shard_map/ppermute | solution.py:17
  469.3 26.3 %copy-start.4 = (f32[1,32,128,256]{3,2,1,0:T(8,128)S(1)}, f32[1,32,128,256]{3,2,1,0:T(8,128)}, u32[]{:S(2)}) copy-start(f32[1,32,128,256]{3,2,1,0:T(8,128)} %param.5) | copy-start | bytes 12582916
  519.2 23.5 %collective-permute-start.6 = (f32[15,128,256]{2,1,0:T(8,128)S(1)}, f32[15,128,256]{2,1,0:T(8,128)S(1)}, u32[]{:S(2)}, u32[]{:S(2)}) collective-permute-start(f32[15,128,256]{2,1,0:T(8,128)S(1)} %get-tuple-element.5), channel_id=1, source_target_pairs={{0,8},{8,16},{16,24},{24,32},{32,40},{40,48},{48,56},{56,64},{64,7... | collective-permute-start | bytes 5898248 | tf_op jit(solution)/shard_map/ppermute | solution.py:16
  521.1 45.5 %collective-permute-start.7 = (f32[15,128,256]{2,1,0:T(8,128)S(1)}, f32[15,128,256]{2,1,0:T(8,128)S(1)}, u32[]{:S(2)}, u32[]{:S(2)}) collective-permute-start(f32[15,128,256]{2,1,0:T(8,128)S(1)} %get-tuple-element.6), channel_id=1, source_target_pairs={{8,0},{16,8},{24,16},{32,24},{40,32},{48,40},{56,48},{64,56},{72,6... | collective-permute-start | bytes 5898248 | tf_op jit(solution)/shard_map/ppermute | solution.py:17
Sparse Core Ops, SparseCore 0:
  281.4 104.2 all-reduce.2
  648.0 101.1 all-reduce.4
where the time goes:
time: 775 us; the launch traced here: 763 us
  waiting for transfers between devices  373 us (48%)
  matrix products  318 us (41%)
  starting transfers between devices  24.8 us (3%)
  other arithmetic  20.8 us (3%)
  between operations  14.1 us (2%)
  local copies, waits for them, and re-layouts  11.8 us (2%)
    psum x2, waiting for transfers between devices, shards(): update = lax.psum(weight * back, 'view')  206 us
    dot_general x4, matrix products, convolve(): volume = jnp.einsum('wz,zyx->wyx', z_matrix, padded, precision=highest)  114 us
    dot_general x4, matrix products, convolve(): volume = jnp.einsum('vy,zyx->zvx', y_matrix, volume, precision=highest)  105 us
    dot_general x4, matrix products, convolve(): return jnp.einsum('wx,zyx->zyw', x_matrix, volume, precision=highest)  99.6 us
    ppermute x4, waiting for transfers between devices, padded_2(): after = lax.ppermute(initial, axis, down)  94.3 us
    ppermute x4, waiting for transfers between devices, padded_2(): before = lax.ppermute(last, axis, up)  72.8 us
  transfers between devices with their start and end apart: 10, of which 10 were waited for; matrix products, arithmetic and copies ran while one was open for 1% of the time, Pallas kernels for 0%

commit v1 on v0

v1 whole, which is shorter than its diff:
```python
import jax
import jax.numpy as jnp
from jax import lax
from jax.experimental import pallas as pl
from jax.experimental.pallas import tpu as pltpu
from jax.sharding import PartitionSpec as P

ITERS = 2
MESH = pl.DeviceIdType.MESH
F32 = jnp.float32
BF16 = jnp.bfloat16

DEPTH = 32
HALO = 15
EXT = DEPTH + 2 * HALO
PAD = 64
ROWS = 128
COLS = 256
HALF = 128
OCTETS = ROWS // 8
TAPS = 31
GROUPS = 8
GROUP = DEPTH // GROUPS
SEMS = 160


def split(value):
    high = value.astype(BF16)
    return high, (value - high.astype(F32)).astype(BF16)


def dot(left, right):
    return jnp.dot(left, right, preferred_element_type=F32)


def from_left(matrix, value):
    high, low = split(value)
    return dot(matrix[0], high) + (dot(matrix[1], high) + dot(matrix[0], low))


def from_right(value, matrix):
    high, low = split(value)
    return dot(high, matrix[0]) + (dot(high, matrix[1]) + dot(low, matrix[0]))


def kernel(
    est, recording, counts, psf, out,
    cur, rec, mid, part, rsib, e_low, e_high, rs_a, rs_b, gat, wb, wraw, wext, wt, pown, pin,
    x_blur, x_back, y_blur, y_back, z_blur, z_back,
    send_sem, recv_sem, load_sem, out_sem,
):
    slab, view = lax.axis_index("slab"), lax.axis_index("view")
    core, pair = lax.rem(slab, 2), slab // 2
    side, row = view // 4, lax.rem(view, 4)
    chip = pair * 2 + side
    native = core == side
    foreign = core != side

    def dev(chip_at, row_at, core_at):
        return ((chip_at // 2) * 2 + core_at, lax.rem(chip_at, 2) * 4 + row_at)

    prev_chip, next_chip = lax.rem(chip + 15, 16), lax.rem(chip + 1, 16)
    partner_chip = pair * 2 + 1 - side
    outer_chip = jnp.where(side == 0, prev_chip, next_chip)
    prev_row, next_row = lax.rem(row + 3, 4), lax.rem(row + 1, 4)
    far_row = lax.rem(row + 2, 4)
    sibling = dev(chip, row, 1 - core)
    low_dev, high_dev = dev(prev_chip, row, core), dev(next_chip, row, core)
    down, up = dev(chip, prev_row, core), dev(chip, next_row, core)
    partner = dev(partner_chip, row, core)
    cross = dev(jnp.where(native, outer_chip, partner_chip), row, 1 - core)

    names = {}

    def sem(name):
        return names.setdefault(name, len(names))

    def copy(name, src, dst, device):
        i = sem(name)
        return pltpu.make_async_remote_copy(
            src_ref=src, dst_ref=dst, send_sem=send_sem.at[i], recv_sem=recv_sem.at[i],
            device_id=device, device_id_type=MESH)

    def send(name, src, dst, device):
        handle = copy(name, src, dst, device)
        handle.start()
        return handle

    def await_recv(name, dst):
        copy(name, dst, dst, sibling).wait_recv()

    barrier = pltpu.get_barrier_semaphore()
    for device in (sibling, low_dev, high_dev, down, up, cross):
        pl.semaphore_signal(barrier, inc=1, device_id=device, device_id_type=MESH)
    pl.semaphore_wait(barrier, 6)

    near = jnp.where(side == 0, EXT - HALO, 0)
    outer = jnp.where(side == 0, 0, EXT - HALO)
    own_edge = jnp.where(side == 0, HALO, DEPTH)
    raw_edge = jnp.where(side == 0, 0, DEPTH - HALO)

    def planes(first, count):
        return cur.at[:, :, pl.ds(first, count)]

    def group(g):
        return rec.at[pl.ds(g * GROUP, GROUP)]

    def rows_of(first, count):
        return wext.at[pl.ds(first, count)]

    @pl.when(foreign)
    def _():
        for g in range(GROUPS):
            send(("rec", g), recording.at[0, pl.ds(g * GROUP, GROUP)], group(g), cross)

    @pl.when(native)
    def _():
        pltpu.make_async_copy(recording.at[0], rec, load_sem.at[1]).start()

        @pl.loop(0, OCTETS)
        def _(octet):
            for half in range(2):
                pltpu.make_async_copy(
                    est.at[:, pl.ds(pl.multiple_of(octet * 8, 8), 8), pl.ds(half * HALF, HALF)],
                    cur.at[half, octet, pl.ds(HALO, DEPTH)], load_sem.at[0]).start()

    @pl.when(foreign)
    def _():
        @pl.loop(0, OCTETS)
        def _(octet):
            for half in range(2):
                pltpu.make_async_copy(
                    est.at[pl.ds(raw_edge, HALO), pl.ds(pl.multiple_of(octet * 8, 8), 8), pl.ds(half * HALF, HALF)],
                    cur.at[half, octet, pl.ds(near, HALO)], load_sem.at[0]).start()

    pown[...] = jnp.zeros_like(pown)
    pown[0:3, 0:TAPS] = psf[0]

    @pl.when(foreign)
    def _():
        send("psf", pown, pin, cross)

    @pl.when(native)
    def _():
        pin[...] = pown[...]

    total = jnp.sum(counts[...].astype(F32), axis=0)
    wraw[...] = jnp.zeros_like(wraw)
    for v in range(2):
        weight = counts[row + 4 * v].astype(F32) / total
        for z in range(DEPTH):
            wraw[z, v:v + 1, :] = weight[z:z + 1, :]

    @pl.when(native)
    def _():
        wext[HALO:HALO + DEPTH] = wraw[...]
        send("w_own", rows_of(HALO, DEPTH), rows_of(HALO, DEPTH), sibling)
        send("w_outer", rows_of(own_edge, HALO), rows_of(near, HALO), cross)
        whole = planes(HALO, DEPTH)
        pltpu.make_async_copy(whole, whole, load_sem.at[0]).wait()
        for k in range(4):
            send(("est_outer", k), cur.at[:, 4 * k:4 * k + 4, pl.ds(own_edge, HALO)],
                 cur.at[:, 4 * k:4 * k + 4, pl.ds(near, HALO)], cross)
        send("est_own", whole, whole, sibling)

    @pl.when(foreign)
    def _():
        wext[pl.ds(near, HALO)] = wraw[pl.ds(raw_edge, HALO)]
        send("w_near", rows_of(near, HALO), rows_of(near, HALO), sibling)
        edge = planes(near, HALO)
        pltpu.make_async_copy(edge, edge, load_sem.at[0]).wait()
        send("est_near", edge, edge, sibling)

    wext[EXT:PAD] = jnp.zeros((PAD - EXT, 8, HALF), F32)

    @pl.loop(0, OCTETS)
    def _(octet):
        for half in range(2):
            cur[half, octet, EXT:PAD] = jnp.zeros((PAD - EXT, 8, HALF), F32)

    @pl.when(foreign)
    def _():
        await_recv("psf", pin)

    taps = pin[0:3, :] / jnp.sum(pin[0:3, :], axis=1, keepdims=True)

    def build(ref, axis, index_of):
        height, width = ref.shape[1:]
        kernel_taps = [taps[axis:axis + 1, t:t + 1] for t in range(TAPS)]

        @pl.loop(0, height // 16)
        def _(block):
            first = pl.multiple_of(block * 16, 16)
            down_at = lax.broadcasted_iota(jnp.int32, (16, width), 0) + first
            across = lax.broadcasted_iota(jnp.int32, (16, width), 1)
            index = index_of(down_at, across)
            value = jnp.zeros((16, width), F32)
            for t in range(TAPS):
                value = jnp.where(index == t, kernel_taps[t], value)
            high, low = split(value)
            ref[0, pl.ds(first, 16), :] = high
            ref[1, pl.ds(first, 16), :] = low

    inside_low = jnp.where(chip == 0, HALO, 0)
    inside_high = jnp.where(chip == 15, HALO + DEPTH, EXT)

    def plane_index(ext_at, own_at):
        ext_plane, own_plane = ext_at // 8, own_at // 8
        fits = (lax.rem(ext_at, 8) == lax.rem(own_at, 8)) & (ext_plane >= inside_low) & (ext_plane < inside_high)
        return fits, ext_plane, own_plane

    def z_blur_index(a, b):
        fits, ext_plane, own_plane = plane_index(b, a)
        return jnp.where(fits, own_plane + 2 * HALO - ext_plane, -1)

    def z_back_index(a, b):
        fits, ext_plane, own_plane = plane_index(a, b)
        return jnp.where(fits, own_plane + 2 * HALO - ext_plane, -1)

    build(z_blur, 0, z_blur_index)
    build(x_blur, 2, lambda a, b: HALO + b - a)
    build(y_blur, 1, lambda a, b: HALO + a - b)
    build(y_back, 1, lambda a, b: HALO + b - a)
    build(x_back, 2, lambda a, b: HALO + a - b)
    build(z_back, 0, z_back_index)

    @pl.when(native)
    def _():
        await_recv("w_outer", rows_of(outer, HALO))
        send("w_outer_on", rows_of(outer, HALO), rows_of(outer, HALO), sibling)
        await_recv("w_near", rows_of(near, HALO))

    @pl.when(foreign)
    def _():
        await_recv("w_own", rows_of(HALO, DEPTH))
        await_recv("w_outer_on", rows_of(outer, HALO))

    own_weight = jnp.where(core == 0, wext[:, 0, :], wext[:, 1, :])
    wt[:, 0:PAD] = own_weight.T

    @pl.loop(0, OCTETS)
    def _(octet):
        block = wt[pl.ds(pl.multiple_of(octet * 8, 8), 8), :]
        for z in range(EXT):
            wb[octet, z] = jnp.broadcast_to(block[:, z:z + 1], (8, HALF))

    def blur_octet(octet):
        value = jnp.concatenate([cur[0, octet].reshape(PAD * 8, HALF), cur[1, octet].reshape(PAD * 8, HALF)], axis=1)
        value = from_left(z_blur, value)
        value = from_right(value, x_blur)
        mid[:, pl.ds(pl.multiple_of(octet * 8, 8), 8), :] = value.reshape(DEPTH, 8, COLS)

    def blur_block(block):
        @pl.loop(0, 2)
        def _(k):
            blur_octet(block * 2 + k)

    def quotient_plane(z):
        value = from_left(y_blur, mid[z])
        value = rec[z] / value
        value = from_left(y_back, value)
        mid[z] = from_right(value, x_back)

    def back_octet(octet):
        value = mid[:, pl.ds(pl.multiple_of(octet * 8, 8), 8), :].reshape(DEPTH * 8, COLS)
        value = from_left(z_back, value).reshape(PAD, 8, COLS)[:EXT]
        weight = wb[octet]
        part[0, octet] = value[:, :, :HALF] * weight
        part[1, octet] = value[:, :, HALF:] * weight

    def back_block(block):
        @pl.loop(0, 2)
        def _(k):
            back_octet(block * 2 + k)

    def both(block):
        return pl.ds(block * 2, 2)

    rs_blocks = [
        (2 * lax.rem(row + 3 - t, 4), 2 * lax.rem(row + 1 + t, 4) + 1) for t in range(4)
    ]

    def reduce_scatter():
        pending = []

        def compute(t):
            for name, block in zip("ab", rs_blocks[t]):
                back_block(block)
                pending.append(send(("sib", t, name), part.at[1 - core, both(block)], rsib.at[both(block)], sibling))

        def edges(t):
            for name, block in zip("ab", rs_blocks[t]):
                await_recv(("sib", t, name), rsib.at[both(block)])

                @pl.loop(0, 2)
                def _(k):
                    octet = block * 2 + k
                    part[core, octet] = part[core, octet] + rsib[octet]

                pending.append(send(("e_high", t, name), part.at[core, both(block), pl.ds(0, HALO)],
                                    e_high.at[both(block)], low_dev))
                pending.append(send(("e_low", t, name), part.at[core, both(block), pl.ds(HALO + DEPTH, HALO)],
                                    e_low.at[both(block)], high_dev))

        def own(t):
            for name, block, ring in zip("ab", rs_blocks[t], (rs_a, rs_b)):
                await_recv(("e_high", t, name), e_high.at[both(block)])
                await_recv(("e_low", t, name), e_low.at[both(block)])
                if t:
                    await_recv(("ring", t - 1, name), ring.at[t - 1])

                @pl.loop(0, 2)
                def _(k):
                    octet = block * 2 + k
                    first, last = pl.ds(HALO, HALO), pl.ds(DEPTH, HALO)
                    part[core, octet, first] = part[core, octet, first] + e_low[octet]
                    part[core, octet, last] = part[core, octet, last] + e_high[octet]
                    if t:
                        middle = pl.ds(HALO, DEPTH)
                        part[core, octet, middle] = part[core, octet, middle] + ring[t - 1, k]
                    if t == 3:
                        middle = pl.ds(HALO, DEPTH)
                        cur[core, octet, middle] = cur[core, octet, middle] * part[core, octet, middle]

                if t < 3:
                    pending.append(send(("ring", t, name), part.at[core, both(block), pl.ds(HALO, DEPTH)],
                                        ring.at[t], up if name == "a" else down))

        compute(0)
        compute(1)
        edges(0)
        compute(2)
        edges(1)
        own(0)
        compute(3)
        edges(2)
        own(1)
        edges(3)
        own(2)
        own(3)
        for handle in pending:
            handle.wait_send()

    def region(half, block, first=0, count=EXT):
        return cur.at[half, both(block), pl.ds(first, count)]

    def middle_of(block):
        return region(core, block, HALO, DEPTH)

    a_own, b_own = 2 * row, 2 * row + 1
    a_prev, b_prev = 2 * prev_row, 2 * prev_row + 1
    a_next, b_next = 2 * next_row, 2 * next_row + 1
    a_far, b_far = 2 * far_row, 2 * far_row + 1
    gather_blocks = [(a_own, b_own), (a_prev, b_next), (b_prev, a_next), (a_far, b_far)]

    def gather_and_blur():
        pending = []

        def pass_on(name, block, device):
            pending.append(send(name, middle_of(block), middle_of(block), device))

        def halos(u):
            for name, block in zip("ab", gather_blocks[u]):
                pending.append(send(("h_high", u, name), region(core, block, HALO, HALO),
                                    region(core, block, HALO + DEPTH, HALO), low_dev))
                pending.append(send(("h_low", u, name), region(core, block, DEPTH, HALO),
                                    region(core, block, 0, HALO), high_dev))

        def share(u):
            for name, block in zip("ab", gather_blocks[u]):
                await_recv(("h_high", u, name), region(core, block, HALO + DEPTH, HALO))
                await_recv(("h_low", u, name), region(core, block, 0, HALO))
                pending.append(send(("share", u, name), region(core, block), region(core, block), sibling))

        def blur(u):
            for name, block in zip("ab", gather_blocks[u]):
                await_recv(("share", u, name), region(1 - core, block))
                blur_block(block)

        pass_on(("y", 1, "a"), a_own, up)
        pass_on(("y", 1, "b"), b_own, down)
        pass_on(("y", 2, "a"), b_own, up)
        pass_on(("y", 2, "b"), a_own, down)
        halos(0)
        await_recv(("y", 1, "a"), middle_of(a_prev))
        await_recv(("y", 1, "b"), middle_of(b_next))
        pass_on(("y", 3, "a"), a_prev, up)
        pass_on(("y", 3, "b"), b_next, down)
        halos(1)
        share(0)
        await_recv(("y", 2, "a"), middle_of(b_prev))
        await_recv(("y", 2, "b"), middle_of(a_next))
        halos(2)
        blur(0)
        share(1)
        await_recv(("y", 3, "a"), middle_of(a_far))
        await_recv(("y", 3, "b"), middle_of(b_far))
        halos(3)
        blur(1)
        share(2)
        blur(2)
        share(3)
        blur(3)
        for handle in pending:
            handle.wait_send()

    lanes = pl.ds(pl.multiple_of(core * HALF, HALF), HALF)

    def final_gather():
        pending = []

        def held(block):
            return gat.at[both(block)]

        def octet_own(octet):
            return cur.at[core, octet, pl.ds(HALO, DEPTH)]

        def to(name, src, dst, device):
            pending.append(send(name, src, dst, device))

        def write(block, own_slab):
            here = native if own_slab else foreign

            def pieces():
                for k in range(2):
                    octet = block * 2 + k
                    src = octet_own(octet) if own_slab else gat.at[octet]
                    yield src, out.at[:, pl.ds(pl.multiple_of(octet * 8, 8), 8), lanes]

            @pl.when(here)
            def _():
                for src, dst in pieces():
                    pltpu.make_async_copy(src, dst, out_sem.at[0]).start()

            @pl.when(jnp.logical_not(here))
            def _():
                for src, dst in pieces():
                    pltpu.make_async_remote_copy(
                        src_ref=src, dst_ref=dst, send_sem=out_sem.at[1], recv_sem=out_sem.at[2],
                        device_id=sibling, device_id_type=MESH).start()

        to(("x", 0), middle_of(a_own), held(a_own), partner)
        to(("by", 0), middle_of(b_own), middle_of(b_own), up)
        to(("by", 1), middle_of(b_own), middle_of(b_own), down)
        to(("x", 1), middle_of(b_own), held(b_own), partner)
        to(("ay", 0), middle_of(a_own), middle_of(a_own), up)
        to(("ay", 1), middle_of(a_own), middle_of(a_own), down)
        write(a_own, True)
        write(b_own, True)
        await_recv(("x", 0), held(a_own))
        to(("gy", 0), held(a_own), held(a_own), up)
        to(("gy", 1), held(a_own), held(a_own), down)
        write(a_own, False)
        await_recv(("by", 0), middle_of(b_prev))
        to(("bf", 0), octet_own(b_prev * 2), octet_own(b_prev * 2), up)
        to(("x", 2), middle_of(b_prev), held(b_prev), partner)
        await_recv(("by", 1), middle_of(b_next))
        to(("bf", 1), octet_own(b_next * 2 + 1), octet_own(b_next * 2 + 1), down)
        to(("x", 3), middle_of(b_next), held(b_next), partner)
        write(b_prev, True)
        write(b_next, True)
        await_recv(("x", 1), held(b_own))
        write(b_own, False)
        await_recv(("ay", 1), middle_of(a_next))
        to(("af", 1), middle_of(a_next), middle_of(a_next), down)
        await_recv(("ay", 0), middle_of(a_prev))
        write(a_next, True)
        write(a_prev, True)
        await_recv(("bf", 0), octet_own(b_far * 2))
        await_recv(("bf", 1), octet_own(b_far * 2 + 1))
        to(("x", 4), middle_of(b_far), held(b_far), partner)
        write(b_far, True)
        await_recv(("gy", 0), held(a_prev))
        to(("gf", 0), held(a_prev), held(a_prev), up)
        await_recv(("gy", 1), held(a_next))
        write(a_prev, False)
        write(a_next, False)
        await_recv(("x", 2), held(b_prev))
        write(b_prev, False)
        await_recv(("x", 3), held(b_next))
        write(b_next, False)
        await_recv(("af", 1), middle_of(a_far))
        write(a_far, True)
        await_recv(("gf", 0), held(a_far))
        write(a_far, False)
        await_recv(("x", 4), held(b_far))
        write(b_far, False)
        for handle in pending:
            handle.wait_send()
        half_out = out.at[:, :, pl.ds(0, HALF)]
        pltpu.make_async_copy(half_out, half_out, out_sem.at[0]).wait()
        final = pltpu.make_async_remote_copy(
            src_ref=half_out, dst_ref=half_out, send_sem=out_sem.at[1], recv_sem=out_sem.at[2],
            device_id=sibling, device_id_type=MESH)
        final.wait_send()
        final.wait_recv()

    @pl.when(native)
    def _():
        await_recv("est_near", planes(near, HALO))

    @pl.when(foreign)
    def _():
        await_recv("est_own", planes(HALO, DEPTH))

    for k in range(4):
        strip = cur.at[:, 4 * k:4 * k + 4, pl.ds(outer, HALO)]

        @pl.when(native)
        def _():
            await_recv(("est_outer", k), strip)
            send(("est_on", k), strip, strip, sibling)

        @pl.when(foreign)
        def _():
            await_recv(("est_on", k), strip)

        @pl.loop(4 * k, 4 * k + 4)
        def _(octet):
            blur_octet(octet)

    @pl.when(native)
    def _():
        pltpu.make_async_copy(recording.at[0], rec, load_sem.at[1]).wait()

    for g in range(GROUPS):
        @pl.when(foreign)
        def _():
            await_recv(("rec", g), group(g))

        @pl.loop(g * GROUP, (g + 1) * GROUP)
        def _(z):
            quotient_plane(z)

    @pl.when(native)
    def _():
        copy("w_own", rows_of(HALO, DEPTH), rows_of(HALO, DEPTH), sibling).wait_send()
        copy("w_outer", rows_of(own_edge, HALO), rows_of(near, HALO), cross).wait_send()
        copy("w_outer_on", rows_of(outer, HALO), rows_of(outer, HALO), sibling).wait_send()
        copy("est_own", planes(HALO, DEPTH), planes(HALO, DEPTH), sibling).wait_send()
        for k in range(4):
            strip = cur.at[:, 4 * k:4 * k + 4, pl.ds(outer, HALO)]
            copy(("est_outer", k), strip, strip, cross).wait_send()
            copy(("est_on", k), strip, strip, sibling).wait_send()

    @pl.when(foreign)
    def _():
        copy("psf", pown, pin, cross).wait_send()
        copy("w_near", rows_of(near, HALO), rows_of(near, HALO), sibling).wait_send()
        copy("est_near", planes(near, HALO), planes(near, HALO), sibling).wait_send()
        for g in range(GROUPS):
            copy(("rec", g), recording.at[0, pl.ds(g * GROUP, GROUP)], group(g), cross).wait_send()

    reduce_scatter()
    for step in range(1, ITERS):
        gather_and_blur()

        @pl.loop(0, DEPTH)
        def _(z):
            quotient_plane(z)

        reduce_scatter()
    final_gather()


def shards(estimate, views_data, counts, psf):
    any_space = pl.BlockSpec(memory_space=pl.ANY)
    vmem = pl.BlockSpec(memory_space=pltpu.VMEM)
    return pl.pallas_call(
        kernel,
        out_shape=jax.ShapeDtypeStruct((DEPTH, ROWS, COLS), F32),
        in_specs=[any_space, any_space, vmem, vmem],
        out_specs=any_space,
        scratch_shapes=[
            pltpu.VMEM((2, OCTETS, PAD, 8, HALF), F32),
            pltpu.VMEM((DEPTH, ROWS, COLS), F32),
            pltpu.VMEM((DEPTH, ROWS, COLS), F32),
            pltpu.VMEM((2, OCTETS, EXT, 8, HALF), F32),
            pltpu.VMEM((OCTETS, EXT, 8, HALF), F32),
            pltpu.VMEM((OCTETS, HALO, 8, HALF), F32),
            pltpu.VMEM((OCTETS, HALO, 8, HALF), F32),
            pltpu.VMEM((3, 2, DEPTH, 8, HALF), F32),
            pltpu.VMEM((3, 2, DEPTH, 8, HALF), F32),
            pltpu.VMEM((OCTETS, DEPTH, 8, HALF), F32),
            pltpu.VMEM((OCTETS, EXT, 8, HALF), F32),
            pltpu.VMEM((DEPTH, 8, HALF), F32),
            pltpu.VMEM((PAD, 8, HALF), F32),
            pltpu.VMEM((ROWS, HALF), F32),
            pltpu.VMEM((8, HALF), F32),
            pltpu.VMEM((8, HALF), F32),
            pltpu.VMEM((2, COLS, COLS), BF16),
            pltpu.VMEM((2, COLS, COLS), BF16),
            pltpu.VMEM((2, ROWS, ROWS), BF16),
            pltpu.VMEM((2, ROWS, ROWS), BF16),
            pltpu.VMEM((2, DEPTH * 8, PAD * 8), BF16),
            pltpu.VMEM((2, PAD * 8, DEPTH * 8), BF16),
            pltpu.SemaphoreType.DMA((SEMS,)),
            pltpu.SemaphoreType.DMA((SEMS,)),
            pltpu.SemaphoreType.DMA((2,)),
            pltpu.SemaphoreType.DMA((3,)),
        ],
        compiler_params=pltpu.CompilerParams(
            collective_id=0, has_side_effects=True, vmem_limit_bytes=60 * 2**20),
        cost_estimate=pl.CostEstimate(flops=2 * 10**10, bytes_accessed=2 * 10**7, transcendentals=0),
    )(estimate, views_data, counts, psf)


def solution(mesh):
    in_specs = (
        P("slab", None, None),
        P("view", "slab", None, None),
        P(None, "slab", None),
        P("view", None, None),
    )
    out_specs = P("slab", None, None)
    return jax.shard_map(shards, mesh=mesh, in_specs=in_specs, out_specs=out_specs, check_vma=False)
```

time: 775 us -> 262 us (0.34); the launches traced: 763 us -> 262 us
  waiting for transfers between devices: 373 us -> 0 us
  matrix products: 318 us -> 0 us
  Pallas kernels: 0 us -> 256 us
  starting transfers between devices: 24.8 us -> 0 us
  other arithmetic: 20.8 us -> 0 us
  between operations: 14.1 us -> 0.01 us
    dot_general x12 -> x0, matrix products: 318 us -> none  [the longest x4 114 us: convolve(): volume = jnp.einsum('wz,zyx->wyx', z_matrix, padded, precision=highest)]
    pallas_call x0 -> x1, Pallas kernels: none -> 256 us  [shards(): pl.pallas_call(kernel, out_shape=jax.ShapeDtypeStruct((DEPTH, ROWS, COLS)...]
    psum x2 -> x0, waiting for transfers between devices: 206 us -> none  [shards(): update = lax.psum(weight * back, 'view')]
    ppermute x8 -> x0, waiting for transfers between devices: 167 us -> none  [the longest x4 94.3 us: padded_2(): after = lax.ppermute(initial, axis, down)]
    ppermute x8 -> x0, starting transfers between devices: 24.8 us -> none  [the longest x4 14.7 us: padded_2(): before = lax.ppermute(last, axis, up)]
    slice x9 -> x0, local copies, waits for them, and re-layouts: 11.8 us -> none  [the longest x4 8.15 us: padded_2(): last = lax.slice_in_dim(value, length - width, length, axis=dim)]
    concatenate x4 -> x0, other arithmetic: 10.3 us -> none  [padded_2(): value = jnp.concatenate([before, value, after], axis=dim)]
    mul x2 -> x0, other arithmetic: 10.3 us -> none  [shards(): current = current * update]
  transfers between devices with their start and end apart: 10 -> 0, of which waited for: 10 -> 0; matrix products, arithmetic and copies ran while one was open for 1% -> 0% of each run, Pallas kernels for 0% -> 0%
where the time goes in v1:
time: 262 us
  Pallas kernels  256 us (98%)
  local copies, waits for them, and re-layouts  5.91 us (2%)
    pallas_call x1, Pallas kernels, shards(): pl.pallas_call(kernel, out_shape=jax.ShapeDtypeStruct((DEPTH, ROWS, COLS)...  256 us
    unnamed x2, local copies, waits for them, and re-layouts  5.91 us

profile of v1, /device:TPU:1, one launch (start us, length us, event | category | flops | bytes accessed | tf_op | source)
XLA Modules:
  0.0 261.7 jit_solution(4463970449939792934)
XLA Ops:
  0.0 1.3 copy.5.psf
  1.3 255.8 %shard_map.46 = f32[32,128,256]{2,1,0:T(8,128)} custom-call(f32[32,128,256]{2,1,0:T(8,128)} %est.1, f32[1,32,128,256]{3,2,1,0:T(8,128)} %recording.1, s32[8,32,128]{2,1,0:T(8,128)} %counts.1, f32[1,3,31]{2,1,0:T(4,128)} %copy.5.psf), custom_call_target="tpu_custom_call" | custom-call | flops 20000000000 | bytes 20000000 | tf_op jit(solution)/shard_map/pallas_call | solution.py:569
  257.0 4.7 %copy.7 = f32[32,128,256]{2,1,0:T(8,128)} copy(f32[32,128,256]{2,1,0:T(8,128)} %shard_map.46) | data formatting | bytes 8388608

commit v2 on v1

--- a/solution.py
+++ b/solution.py
@@ -35,12 +35,30 @@
 
 def from_left(matrix, value):
     high, low = split(value)
-    return dot(matrix[0], high) + (dot(matrix[1], high) + dot(matrix[0], low))
+    both = jnp.concatenate([matrix[0], matrix[0]], axis=1)
+    return dot(both, jnp.concatenate([high, low], axis=0)) + dot(matrix[1], high)
 
 
 def from_right(value, matrix):
     high, low = split(value)
-    return dot(high, matrix[0]) + (dot(high, matrix[1]) + dot(low, matrix[0]))
+    both = jnp.concatenate([matrix[0], matrix[0]], axis=0)
+    return dot(jnp.concatenate([high, low], axis=1), both) + dot(high, matrix[1])
+
+
+def from_left_all(matrix, values):
+    width = values[0].shape[1]
+    high, low = split(jnp.concatenate(values, axis=1))
+    left = jnp.concatenate([matrix[0], matrix[1], matrix[0]], axis=1)
+    result = dot(left, jnp.concatenate([high, high, low], axis=0))
+    return [result[:, width * k:width * (k + 1)] for k in range(len(values))]
+
+
+def from_right_all(values, matrix):
+    height = values[0].shape[0]
+    high, low = split(jnp.concatenate(values, axis=0))
+    right = jnp.concatenate([matrix[0], matrix[1], matrix[0]], axis=0)
+    result = dot(jnp.concatenate([high, high, low], axis=1), right)
+    return [result[height * k:height * (k + 1)] for k in range(len(values))]
 
 
 def kernel(
@@ -108,13 +126,18 @@
     def rows_of(first, count):
         return wext.at[pl.ds(first, count)]
 
+    pown[...] = jnp.zeros_like(pown)
+    pown[0:3, 0:TAPS] = psf[0]
+
     @pl.when(foreign)
     def _():
+        send("psf", pown, pin, cross)
         for g in range(GROUPS):
             send(("rec", g), recording.at[0, pl.ds(g * GROUP, GROUP)], group(g), cross)
 
     @pl.when(native)
     def _():
+        pin[...] = pown[...]
         pltpu.make_async_copy(recording.at[0], rec, load_sem.at[1]).start()
 
         @pl.loop(0, OCTETS)
@@ -132,17 +155,6 @@
                 pltpu.make_async_copy(
                     est.at[pl.ds(raw_edge, HALO), pl.ds(pl.multiple_of(octet * 8, 8), 8), pl.ds(half * HALF, HALF)],
                     cur.at[half, octet, pl.ds(near, HALO)], load_sem.at[0]).start()
-
-    pown[...] = jnp.zeros_like(pown)
-    pown[0:3, 0:TAPS] = psf[0]
-
-    @pl.when(foreign)
-    def _():
-        send("psf", pown, pin, cross)
-
-    @pl.when(native)
-    def _():
-        pin[...] = pown[...]
 
     total = jnp.sum(counts[...].astype(F32), axis=0)
     wraw[...] = jnp.zeros_like(wraw)
@@ -244,34 +256,38 @@
         for z in range(EXT):
             wb[octet, z] = jnp.broadcast_to(block[:, z:z + 1], (8, HALF))
 
-    def blur_octet(octet):
-        value = jnp.concatenate([cur[0, octet].reshape(PAD * 8, HALF), cur[1, octet].reshape(PAD * 8, HALF)], axis=1)
-        value = from_left(z_blur, value)
-        value = from_right(value, x_blur)
-        mid[:, pl.ds(pl.multiple_of(octet * 8, 8), 8), :] = value.reshape(DEPTH, 8, COLS)
-
-    def blur_block(block):
-        @pl.loop(0, 2)
+    def octet_rows(octet):
+        return pl.ds(pl.multiple_of(octet * 8, 8), 8)
+
+    def blur_octets(octets):
+        values = [
+            jnp.concatenate([cur[half, octet].reshape(PAD * 8, HALF) for half in range(2)], axis=1) for octet in octets
+        ]
+        values = from_right_all(from_left_all(z_blur, values), x_blur)
+        for octet, value in zip(octets, values):
+            mid[:, octet_rows(octet), :] = value.reshape(DEPTH, 8, COLS)
+
+    def quotient_planes(first, count):
+        @pl.loop(0, count // 4)
         def _(k):
-            blur_octet(block * 2 + k)
-
-    def quotient_plane(z):
-        value = from_left(y_blur, mid[z])
-        value = rec[z] / value
-        value = from_left(y_back, value)
-        mid[z] = from_right(value, x_back)
-
-    def back_octet(octet):
-        value = mid[:, pl.ds(pl.multiple_of(octet * 8, 8), 8), :].reshape(DEPTH * 8, COLS)
-        value = from_left(z_back, value).reshape(PAD, 8, COLS)[:EXT]
-        weight = wb[octet]
-        part[0, octet] = value[:, :, :HALF] * weight
-        part[1, octet] = value[:, :, HALF:] * weight
-
-    def back_block(block):
-        @pl.loop(0, 2)
-        def _(k):
-            back_octet(block * 2 + k)
+            at = [first + 4 * k + i for i in range(4)]
+            values = [from_left(y_blur, mid[z]) for z in at]
+            values = [rec[z] / value for z, value in zip(at, values)]
+            values = [from_left(y_back, value) for value in values]
+            values = [from_right(value, x_back) for value in values]
+            for z, value in zip(at, values):
+                mid[z] = value
+
+    def back_octets(octets):
+        values = [mid[:, octet_rows(octet), :].reshape(DEPTH * 8, COLS) for octet in octets]
+        for octet, value in zip(octets, from_left_all(z_back, values)):
+            value = value.reshape(PAD, 8, COLS)[:EXT]
+            weight = wb[octet]
+            part[0, octet] = value[:, :, :HALF] * weight
+            part[1, octet] = value[:, :, HALF:] * weight
+
+    def octets_of(blocks):
+        return [block * 2 + k for block in blocks for k in range(2)]
 
     def both(block):
         return pl.ds(block * 2, 2)
@@ -284,8 +300,8 @@
         pending = []
 
         def compute(t):
+            back_octets(octets_of(rs_blocks[t]))
             for name, block in zip("ab", rs_blocks[t]):
-                back_block(block)
                 pending.append(send(("sib", t, name), part.at[1 - core, both(block)], rsib.at[both(block)], sibling))
 
         def edges(t):
@@ -375,7 +391,7 @@
         def blur(u):
             for name, block in zip("ab", gather_blocks[u]):
                 await_recv(("share", u, name), region(1 - core, block))
-                blur_block(block)
+            blur_octets(octets_of(gather_blocks[u]))
 
         pass_on(("y", 1, "a"), a_own, up)
         pass_on(("y", 1, "b"), b_own, down)
@@ -515,9 +531,7 @@
         def _():
             await_recv(("est_on", k), strip)
 
-        @pl.loop(4 * k, 4 * k + 4)
-        def _(octet):
-            blur_octet(octet)
+        blur_octets([4 * k + i for i in range(4)])
 
     @pl.when(native)
     def _():
@@ -528,9 +542,7 @@
         def _():
             await_recv(("rec", g), group(g))
 
-        @pl.loop(g * GROUP, (g + 1) * GROUP)
-        def _(z):
-            quotient_plane(z)
+        quotient_planes(g * GROUP, GROUP)
 
     @pl.when(native)
     def _():
@@ -554,11 +566,7 @@
     reduce_scatter()
     for step in range(1, ITERS):
         gather_and_blur()
-
-        @pl.loop(0, DEPTH)
-        def _(z):
-            quotient_plane(z)
-
+        quotient_planes(0, DEPTH)
         reduce_scatter()
     final_gather()
 

time: 262 us -> 200 us (0.76)
  Pallas kernels: 256 us -> 194 us
    pallas_call x1, Pallas kernels: 256 us -> 194 us  [shards(): pl.pallas_call(kernel, out_shape=jax.ShapeDtypeStruct((DEPTH, ROWS, COLS)...]
where the time goes in v2:
time: 200 us
  Pallas kernels  194 us (97%)
  local copies, waits for them, and re-layouts  5.91 us (3%)
    pallas_call x1, Pallas kernels, shards(): pl.pallas_call(kernel, out_shape=jax.ShapeDtypeStruct((DEPTH, ROWS, COLS)...  194 us
    unnamed x2, local copies, waits for them, and re-layouts  5.91 us

profile of v2, /device:TPU:1, one launch (start us, length us, event | category | flops | bytes accessed | tf_op | source)
XLA Modules:
  0.0 200.1 jit_solution(1128811019349180166)
XLA Ops:
  0.0 1.3 copy.5.psf
  1.3 194.2 %shard_map.46 = f32[32,128,256]{2,1,0:T(8,128)} custom-call(f32[32,128,256]{2,1,0:T(8,128)} %est.1, f32[1,32,128,256]{3,2,1,0:T(8,128)} %recording.1, s32[8,32,128]{2,1,0:T(8,128)} %counts.1, f32[1,3,31]{2,1,0:T(4,128)} %copy.5.psf), custom_call_target="tpu_custom_call" | custom-call | flops 20000000000 | bytes 20000000 | tf_op jit(solution)/shard_map/pallas_call | solution.py:577
  195.4 4.7 %copy.7 = f32[32,128,256]{2,1,0:T(8,128)} copy(f32[32,128,256]{2,1,0:T(8,128)} %shard_map.46) | data formatting | bytes 8388608

commit v3 on v2

--- a/solution.py
+++ b/solution.py
@@ -286,82 +286,64 @@
             part[0, octet] = value[:, :, :HALF] * weight
             part[1, octet] = value[:, :, HALF:] * weight
 
-    def octets_of(blocks):
-        return [block * 2 + k for block in blocks for k in range(2)]
-
-    def both(block):
-        return pl.ds(block * 2, 2)
-
     rs_blocks = [
         (2 * lax.rem(row + 3 - t, 4), 2 * lax.rem(row + 1 + t, 4) + 1) for t in range(4)
     ]
 
+    def unit(blocks, n):
+        return [(name, block * 2 + n % 2) for name, block in zip("ab", blocks[n // 2])]
+
+    first, last, middle = pl.ds(HALO, HALO), pl.ds(DEPTH, HALO), pl.ds(HALO, DEPTH)
+
     def reduce_scatter():
         pending = []
 
-        def compute(t):
-            back_octets(octets_of(rs_blocks[t]))
-            for name, block in zip("ab", rs_blocks[t]):
-                pending.append(send(("sib", t, name), part.at[1 - core, both(block)], rsib.at[both(block)], sibling))
-
-        def edges(t):
-            for name, block in zip("ab", rs_blocks[t]):
-                await_recv(("sib", t, name), rsib.at[both(block)])
-
-                @pl.loop(0, 2)
-                def _(k):
-                    octet = block * 2 + k
-                    part[core, octet] = part[core, octet] + rsib[octet]
-
-                pending.append(send(("e_high", t, name), part.at[core, both(block), pl.ds(0, HALO)],
-                                    e_high.at[both(block)], low_dev))
-                pending.append(send(("e_low", t, name), part.at[core, both(block), pl.ds(HALO + DEPTH, HALO)],
-                                    e_low.at[both(block)], high_dev))
-
-        def own(t):
-            for name, block, ring in zip("ab", rs_blocks[t], (rs_a, rs_b)):
-                await_recv(("e_high", t, name), e_high.at[both(block)])
-                await_recv(("e_low", t, name), e_low.at[both(block)])
+        def to(name, src, dst, device):
+            pending.append(send(name, src, dst, device))
+
+        def compute(n):
+            pairs = unit(rs_blocks, n)
+            back_octets([octet for _, octet in pairs])
+            for name, octet in pairs:
+                to(("sib", n, name), part.at[1 - core, octet], rsib.at[octet], sibling)
+
+        def edges(n):
+            for name, octet in unit(rs_blocks, n):
+                await_recv(("sib", n, name), rsib.at[octet])
+                part[core, octet] = part[core, octet] + rsib[octet]
+                to(("e_high", n, name), part.at[core, octet, pl.ds(0, HALO)], e_high.at[octet], low_dev)
+                to(("e_low", n, name), part.at[core, octet, pl.ds(HALO + DEPTH, HALO)], e_low.at[octet], high_dev)
+
+        def own(n):
+            t, k = n // 2, n % 2
+            for (name, octet), ring in zip(unit(rs_blocks, n), (rs_a, rs_b)):
+                await_recv(("e_high", n, name), e_high.at[octet])
+                await_recv(("e_low", n, name), e_low.at[octet])
                 if t:
-                    await_recv(("ring", t - 1, name), ring.at[t - 1])
-
-                @pl.loop(0, 2)
-                def _(k):
-                    octet = block * 2 + k
-                    first, last = pl.ds(HALO, HALO), pl.ds(DEPTH, HALO)
-                    part[core, octet, first] = part[core, octet, first] + e_low[octet]
-                    part[core, octet, last] = part[core, octet, last] + e_high[octet]
-                    if t:
-                        middle = pl.ds(HALO, DEPTH)
-                        part[core, octet, middle] = part[core, octet, middle] + ring[t - 1, k]
-                    if t == 3:
-                        middle = pl.ds(HALO, DEPTH)
-                        cur[core, octet, middle] = cur[core, octet, middle] * part[core, octet, middle]
-
+                    await_recv(("ring", n - 2, name), ring.at[t - 1, k])
+                part[core, octet, first] = part[core, octet, first] + e_low[octet]
+                part[core, octet, last] = part[core, octet, last] + e_high[octet]
+                if t:
+                    part[core, octet, middle] = part[core, octet, middle] + ring[t - 1, k]
                 if t < 3:
-                    pending.append(send(("ring", t, name), part.at[core, both(block), pl.ds(HALO, DEPTH)],
-                                        ring.at[t], up if name == "a" else down))
-
-        compute(0)
-        compute(1)
-        edges(0)
-        compute(2)
-        edges(1)
-        own(0)
-        compute(3)
-        edges(2)
-        own(1)
-        edges(3)
-        own(2)
-        own(3)
-        for handle in pending:
-            handle.wait_send()
-
-    def region(half, block, first=0, count=EXT):
-        return cur.at[half, both(block), pl.ds(first, count)]
-
-    def middle_of(block):
-        return region(core, block, HALO, DEPTH)
+                    to(("ring", n, name), part.at[core, octet, middle], ring.at[t, k], up if name == "a" else down)
+                else:
+                    cur[core, octet, middle] = cur[core, octet, middle] * part[core, octet, middle]
+
+        for n in range(12):
+            if n < 8:
+                compute(n)
+            if 2 <= n < 10:
+                edges(n - 2)
+            if n >= 4:
+                own(n - 4)
+        return pending
+
+    def region(half, octet, start=0, count=EXT):
+        return cur.at[half, octet, pl.ds(start, count)]
+
+    def middle_of(octet):
+        return region(core, octet, HALO, DEPTH)
 
     a_own, b_own = 2 * row, 2 * row + 1
     a_prev, b_prev = 2 * prev_row, 2 * prev_row + 1
@@ -369,64 +351,66 @@
     a_far, b_far = 2 * far_row, 2 * far_row + 1
     gather_blocks = [(a_own, b_own), (a_prev, b_next), (b_prev, a_next), (a_far, b_far)]
 
-    def gather_and_blur():
-        pending = []
-
-        def pass_on(name, block, device):
-            pending.append(send(name, middle_of(block), middle_of(block), device))
-
-        def halos(u):
-            for name, block in zip("ab", gather_blocks[u]):
-                pending.append(send(("h_high", u, name), region(core, block, HALO, HALO),
-                                    region(core, block, HALO + DEPTH, HALO), low_dev))
-                pending.append(send(("h_low", u, name), region(core, block, DEPTH, HALO),
-                                    region(core, block, 0, HALO), high_dev))
-
-        def share(u):
-            for name, block in zip("ab", gather_blocks[u]):
-                await_recv(("h_high", u, name), region(core, block, HALO + DEPTH, HALO))
-                await_recv(("h_low", u, name), region(core, block, 0, HALO))
-                pending.append(send(("share", u, name), region(core, block), region(core, block), sibling))
-
-        def blur(u):
-            for name, block in zip("ab", gather_blocks[u]):
-                await_recv(("share", u, name), region(1 - core, block))
-            blur_octets(octets_of(gather_blocks[u]))
-
-        pass_on(("y", 1, "a"), a_own, up)
-        pass_on(("y", 1, "b"), b_own, down)
-        pass_on(("y", 2, "a"), b_own, up)
-        pass_on(("y", 2, "b"), a_own, down)
+    def gather_and_blur(pending):
+        def to(name, src, dst, device):
+            pending.append(send(name, src, dst, device))
+
+        def pass_on(n, name, octet, device):
+            to(("y", n, name), middle_of(octet), middle_of(octet), device)
+
+        def halos(n):
+            for name, octet in unit(gather_blocks, n):
+                if n > 1:
+                    await_recv(("y", n, name), middle_of(octet))
+                if n in (2, 3):
+                    pass_on(n + 4, name, octet, up if name == "a" else down)
+                to(("h_high", n, name), region(core, octet, HALO, HALO), region(core, octet, HALO + DEPTH, HALO), low_dev)
+                to(("h_low", n, name), region(core, octet, DEPTH, HALO), region(core, octet, 0, HALO), high_dev)
+
+        def share(n):
+            for name, octet in unit(gather_blocks, n):
+                await_recv(("h_high", n, name), region(core, octet, HALO + DEPTH, HALO))
+                await_recv(("h_low", n, name), region(core, octet, 0, HALO))
+                to(("share", n, name), region(core, octet), region(core, octet), sibling)
+
+        def blur(n):
+            pairs = unit(gather_blocks, n)
+            for name, octet in pairs:
+                await_recv(("share", n, name), region(1 - core, octet))
+            blur_octets([octet for _, octet in pairs])
+
+        for k in range(2):
+            pass_on(2 + k, "a", a_own * 2 + k, up)
+            pass_on(2 + k, "b", b_own * 2 + k, down)
         halos(0)
-        await_recv(("y", 1, "a"), middle_of(a_prev))
-        await_recv(("y", 1, "b"), middle_of(b_next))
-        pass_on(("y", 3, "a"), a_prev, up)
-        pass_on(("y", 3, "b"), b_next, down)
         halos(1)
-        share(0)
-        await_recv(("y", 2, "a"), middle_of(b_prev))
-        await_recv(("y", 2, "b"), middle_of(a_next))
-        halos(2)
-        blur(0)
-        share(1)
-        await_recv(("y", 3, "a"), middle_of(a_far))
-        await_recv(("y", 3, "b"), middle_of(b_far))
-        halos(3)
-        blur(1)
-        share(2)
-        blur(2)
-        share(3)
-        blur(3)
+        for k in range(2):
+            pass_on(4 + k, "a", b_own * 2 + k, up)
+            pass_on(4 + k, "b", a_own * 2 + k, down)
+        for n in range(2, 12):
+            if n < 8:
+                halos(n)
+            if 2 <= n < 10:
+                share(n - 2)
+            if n >= 4:
+                blur(n - 4)
+        return pending
+
+    def finish(pending):
         for handle in pending:
             handle.wait_send()
 
     lanes = pl.ds(pl.multiple_of(core * HALF, HALF), HALF)
 
-    def final_gather():
-        pending = []
+    def final_gather(pending):
+        def both(block):
+            return pl.ds(block * 2, 2)
 
         def held(block):
             return gat.at[both(block)]
+
+        def middle_of(block):
+            return cur.at[core, both(block), pl.ds(HALO, DEPTH)]
 
         def octet_own(octet):
             return cur.at[core, octet, pl.ds(HALO, DEPTH)]
@@ -563,21 +547,23 @@
         for g in range(GROUPS):
             copy(("rec", g), recording.at[0, pl.ds(g * GROUP, GROUP)], group(g), cross).wait_send()
 
-    reduce_scatter()
+    sent = reduce_scatter()
     for step in range(1, ITERS):
-        gather_and_blur()
+        sent = gather_and_blur(sent)
         quotient_planes(0, DEPTH)
-        reduce_scatter()
-    final_gather()
+        finish(sent)
+        sent = reduce_scatter()
+    final_gather(sent)
 
 
 def shards(estimate, views_data, counts, psf):
     any_space = pl.BlockSpec(memory_space=pl.ANY)
+    hbm = pl.BlockSpec(memory_space=pltpu.HBM)
     vmem = pl.BlockSpec(memory_space=pltpu.VMEM)
     return pl.pallas_call(
         kernel,
         out_shape=jax.ShapeDtypeStruct((DEPTH, ROWS, COLS), F32),
-        in_specs=[any_space, any_space, vmem, vmem],
+        in_specs=[hbm, hbm, vmem, vmem],
         out_specs=any_space,
         scratch_shapes=[
             pltpu.VMEM((2, OCTETS, PAD, 8, HALF), F32),
@@ -608,7 +594,7 @@
             pltpu.SemaphoreType.DMA((3,)),
         ],
         compiler_params=pltpu.CompilerParams(
-            collective_id=0, has_side_effects=True, vmem_limit_bytes=60 * 2**20),
+            collective_id=0, has_side_effects=True, vmem_limit_bytes=47 * 2**20),
         cost_estimate=pl.CostEstimate(flops=2 * 10**10, bytes_accessed=2 * 10**7, transcendentals=0),
     )(estimate, views_data, counts, psf)
 

time: 200 us -> 182 us (0.910)
  Pallas kernels: 194 us -> 178 us
  local copies, waits for them, and re-layouts: 5.91 us -> 3.6 us
    pallas_call x1, Pallas kernels: 194 us -> 178 us  [shards(): pl.pallas_call(kernel, out_shape=jax.ShapeDtypeStruct((DEPTH, ROWS, COLS)...]
    unnamed x2 -> x4, local copies, waits for them, and re-layouts: 5.91 us -> 3.6 us
where the time goes in v3:
time: 182 us; the launch traced here: 181 us
  Pallas kernels  178 us (98%)
  local copies, waits for them, and re-layouts  3.6 us (2%)
    pallas_call x1, Pallas kernels, shards(): pl.pallas_call(kernel, out_shape=jax.ShapeDtypeStruct((DEPTH, ROWS, COLS)...  178 us

profile of v3, /device:TPU:1, one launch (start us, length us, event | category | flops | bytes accessed | tf_op | source)
XLA Modules:
  0.0 181.3 jit_solution(3771819584571897835)
XLA Ops:
  0.0 0.7 copy.5.psf
  0.7 0.0 copy-start
  0.7 0.9 copy-done
  1.6 177.7 %shard_map.46 = f32[32,128,256]{2,1,0:T(8,128)S(1)} custom-call(f32[32,128,256]{2,1,0:T(8,128)} %est.1, f32[1,32,128,256]{3,2,1,0:T(8,128)} %recording.1, s32[8,32,128]{2,1,0:T(8,128)S(1)} %copy-done, f32[1,3,31]{2,1,0:T(4,128)S(1)} %copy.5.psf), custom_call_target="tpu_custom_call" | custom-call | flops 20000000000 | bytes 20000000 | tf_op jit(solution)/shard_map/pallas_call | solution.py:563
  179.3 2.0 %copy.7 = f32[32,128,256]{2,1,0:T(8,128)} copy(f32[32,128,256]{2,1,0:T(8,128)S(1)} %shard_map.46) | data formatting | bytes 8388608
Async XLA Ops:
  0.7 0.9 copy-start

commit v4 on v3

--- a/solution.py
+++ b/solution.py
@@ -21,7 +21,41 @@
 TAPS = 31
 GROUPS = 8
 GROUP = DEPTH // GROUPS
-SEMS = 160
+SEMS = 200
+FORWARDED = ((0, "a"), (0, "b"), )
+
+GATHER_ORDER = (
+    ("C", 0, 0, ""), ("C", 0, 1, ""), ("E", 0, 0, "a"), ("E", 0, 0, "b"), ("E", 0, 1, "a"), ("C", 2, 0, ""),
+    ("C", 1, 0, ""), ("C", 1, 1, ""), ("E", 0, 1, "b"), ("O", 0, 0, "a"), ("E", 1, 0, "a"), ("E", 1, 0, "b"),
+    ("E", 1, 1, "a"), ("O", 0, 0, "b"), ("C", 3, 1, ""), ("O", 0, 1, "a"), ("O", 0, 1, "b"), ("E", 1, 1, "b"),
+    ("C", 2, 1, ""), ("E", 2, 0, "a"), ("O", 1, 0, "a"), ("E", 2, 0, "b"), ("E", 2, 1, "a"), ("O", 1, 0, "b"),
+    ("O", 1, 1, "a"), ("E", 2, 1, "b"), ("O", 1, 1, "b"), ("C", 3, 0, ""), ("O", 2, 0, "a"), ("E", 3, 0, "a"),
+    ("O", 2, 0, "b"), ("E", 3, 0, "b"), ("E", 3, 1, "a"), ("O", 2, 1, "a"), ("O", 2, 1, "b"), ("E", 3, 1, "b"),
+    ("O", 3, 0, "a"), ("Y", 1, 0, "a"), ("H", 0, 0, "a"), ("O", 3, 0, "b"), ("Y", 1, 0, "b"), ("H", 0, 0, "b"),
+    ("Y", 2, 0, "a"), ("O", 3, 1, "b"), ("Y", 1, 1, "b"), ("Y", 2, 0, "b"), ("O", 3, 1, "a"), ("H", 0, 1, "b"),
+    ("Y", 1, 1, "a"), ("Y", 2, 1, "a"), ("H", 1, 0, "a"), ("S", 0, 0, "b"), ("H", 0, 1, "a"), ("H", 2, 0, "a"),
+    ("Y", 2, 1, "b"), ("H", 1, 1, "b"), ("S", 0, 0, "a"), ("H", 1, 0, "b"), ("B", 0, 0, ""), ("H", 1, 1, "a"),
+    ("F", 1, 0, "a"), ("H", 2, 0, "b"), ("H", 2, 1, "a"), ("S", 0, 1, "b"), ("S", 0, 1, "a"), ("S", 1, 0, "a"),
+    ("S", 1, 1, "b"), ("H", 2, 1, "b"), ("H", 3, 0, "a"), ("F", 1, 0, "b"), ("S", 1, 0, "b"), ("B", 0, 1, ""),
+    ("H", 3, 1, "b"), ("S", 1, 1, "a"), ("H", 3, 1, "a"), ("S", 2, 0, "a"), ("S", 2, 0, "b"), ("B", 1, 1, ""),
+    ("B", 1, 0, ""), ("H", 3, 0, "b"), ("S", 2, 1, "b"), ("S", 2, 1, "a"), ("S", 3, 0, "a"), ("B", 2, 0, ""),
+    ("S", 3, 1, "b"), ("S", 3, 0, "b"), ("B", 2, 1, ""), ("S", 3, 1, "a"), ("B", 3, 0, ""), ("B", 3, 1, ""),
+)
+
+FINISH_ORDER = (
+    ("C", 0, 1, ""), ("C", 0, 0, ""), ("E", 0, 1, "a"), ("E", 0, 1, "b"), ("C", 2, 0, ""), ("C", 1, 1, ""),
+    ("E", 0, 0, "a"), ("E", 0, 0, "b"), ("O", 0, 1, "a"), ("E", 1, 1, "a"), ("C", 2, 1, ""), ("E", 1, 1, "b"),
+    ("C", 1, 0, ""), ("O", 0, 1, "b"), ("O", 0, 0, "a"), ("E", 1, 0, "a"), ("E", 1, 0, "b"), ("E", 2, 1, "a"),
+    ("C", 3, 1, ""), ("O", 0, 0, "b"), ("E", 2, 0, "a"), ("O", 1, 1, "a"), ("E", 2, 1, "b"), ("O", 1, 1, "b"),
+    ("O", 1, 0, "a"), ("E", 2, 0, "b"), ("E", 3, 1, "a"), ("O", 1, 0, "b"), ("O", 2, 1, "a"), ("E", 3, 1, "b"),
+    ("C", 3, 0, ""), ("O", 2, 1, "b"), ("E", 3, 0, "a"), ("O", 2, 0, "a"), ("E", 3, 0, "b"), ("O", 2, 0, "b"),
+    ("O", 3, 1, "a"), ("ya+", 0, 1, ""), ("xa", 0, 1, ""), ("O", 3, 1, "b"), ("yb+", 0, 1, ""), ("yb-", 0, 1, ""),
+    ("O", 3, 0, "a"), ("xa", 0, 0, ""), ("O", 3, 0, "b"), ("xb", 0, 1, ""), ("yb-", 0, 0, ""), ("yb+", 0, 0, ""),
+    ("g+", 0, 1, ""), ("ya-", 0, 1, ""), ("fb", 0, 1, ""), ("xb", 0, 0, ""), ("xbn", 0, 1, ""), ("xbn", 0, 0, ""),
+    ("g+", 0, 0, ""), ("ya+", 0, 0, ""), ("fa", 0, 1, ""), ("xbp", 0, 0, ""), ("fb", 0, 0, ""), ("ya-", 0, 0, ""),
+    ("xbp", 0, 1, ""), ("g-", 0, 1, ""), ("g-", 0, 0, ""), ("gf", 0, 0, ""), ("gf", 0, 1, ""), ("fa", 0, 0, ""),
+    ("xbf", 0, 1, ""), ("gb", 0, 0, ""),
+)
 
 
 def split(value):
@@ -62,8 +96,8 @@
 
 
 def kernel(
-    est, recording, counts, psf, out,
-    cur, rec, mid, part, rsib, e_low, e_high, rs_a, rs_b, gat, wb, wraw, wext, wt, pown, pin,
+    est, recording, counts_in, psf, out,
+    counts, cur, rec, mid, part, rsib, e_low, e_high, rs_a, rs_b, gat, wb, wraw, wext, wt, pown, pin,
     x_blur, x_back, y_blur, y_back, z_blur, z_back,
     send_sem, recv_sem, load_sem, out_sem,
 ):
@@ -107,6 +141,7 @@
     def await_recv(name, dst):
         copy(name, dst, dst, sibling).wait_recv()
 
+    pltpu.make_async_copy(counts_in, counts, load_sem.at[2]).start()
     barrier = pltpu.get_barrier_semaphore()
     for device in (sibling, low_dev, high_dev, down, up, cross):
         pl.semaphore_signal(barrier, inc=1, device_id=device, device_id_type=MESH)
@@ -127,7 +162,8 @@
         return wext.at[pl.ds(first, count)]
 
     pown[...] = jnp.zeros_like(pown)
-    pown[0:3, 0:TAPS] = psf[0]
+    for axis in range(3):
+        pown[axis:axis + 1, 0:TAPS] = psf[axis]
 
     @pl.when(foreign)
     def _():
@@ -156,6 +192,7 @@
                     est.at[pl.ds(raw_edge, HALO), pl.ds(pl.multiple_of(octet * 8, 8), 8), pl.ds(half * HALF, HALF)],
                     cur.at[half, octet, pl.ds(near, HALO)], load_sem.at[0]).start()
 
+    pltpu.make_async_copy(counts_in, counts, load_sem.at[2]).wait()
     total = jnp.sum(counts[...].astype(F32), axis=0)
     wraw[...] = jnp.zeros_like(wraw)
     for v in range(2):
@@ -290,54 +327,48 @@
         (2 * lax.rem(row + 3 - t, 4), 2 * lax.rem(row + 1 + t, 4) + 1) for t in range(4)
     ]
 
-    def unit(blocks, n):
-        return [(name, block * 2 + n % 2) for name, block in zip("ab", blocks[n // 2])]
+    def unit(blocks, t, k):
+        return [(name, block * 2 + k) for name, block in zip("ab", blocks[t])]
 
     first, last, middle = pl.ds(HALO, HALO), pl.ds(DEPTH, HALO), pl.ds(HALO, DEPTH)
-
-    def reduce_scatter():
-        pending = []
-
-        def to(name, src, dst, device):
-            pending.append(send(name, src, dst, device))
-
-        def compute(n):
-            pairs = unit(rs_blocks, n)
-            back_octets([octet for _, octet in pairs])
-            for name, octet in pairs:
-                to(("sib", n, name), part.at[1 - core, octet], rsib.at[octet], sibling)
-
-        def edges(n):
-            for name, octet in unit(rs_blocks, n):
-                await_recv(("sib", n, name), rsib.at[octet])
-                part[core, octet] = part[core, octet] + rsib[octet]
-                to(("e_high", n, name), part.at[core, octet, pl.ds(0, HALO)], e_high.at[octet], low_dev)
-                to(("e_low", n, name), part.at[core, octet, pl.ds(HALO + DEPTH, HALO)], e_low.at[octet], high_dev)
-
-        def own(n):
-            t, k = n // 2, n % 2
-            for (name, octet), ring in zip(unit(rs_blocks, n), (rs_a, rs_b)):
-                await_recv(("e_high", n, name), e_high.at[octet])
-                await_recv(("e_low", n, name), e_low.at[octet])
-                if t:
-                    await_recv(("ring", n - 2, name), ring.at[t - 1, k])
-                part[core, octet, first] = part[core, octet, first] + e_low[octet]
-                part[core, octet, last] = part[core, octet, last] + e_high[octet]
-                if t:
-                    part[core, octet, middle] = part[core, octet, middle] + ring[t - 1, k]
-                if t < 3:
-                    to(("ring", n, name), part.at[core, octet, middle], ring.at[t, k], up if name == "a" else down)
-                else:
-                    cur[core, octet, middle] = cur[core, octet, middle] * part[core, octet, middle]
-
-        for n in range(12):
-            if n < 8:
-                compute(n)
-            if 2 <= n < 10:
-                edges(n - 2)
-            if n >= 4:
-                own(n - 4)
-        return pending
+    pending = []
+
+    def to(name, src, dst, device):
+        pending.append(send(name, src, dst, device))
+
+    def finish():
+        for handle in pending:
+            handle.wait_send()
+        pending.clear()
+
+    def compute(t, k, _):
+        pairs = unit(rs_blocks, t, k)
+        back_octets([octet for _, octet in pairs])
+        for name, octet in pairs:
+            to(("sib", t, k, name), part.at[1 - core, octet], rsib.at[octet], sibling)
+
+    def edges(t, k, name):
+        octet = dict(unit(rs_blocks, t, k))[name]
+        await_recv(("sib", t, k, name), rsib.at[octet])
+        part[core, octet] = part[core, octet] + rsib[octet]
+        to(("e_high", t, k, name), part.at[core, octet, pl.ds(0, HALO)], e_high.at[octet], low_dev)
+        to(("e_low", t, k, name), part.at[core, octet, pl.ds(HALO + DEPTH, HALO)], e_low.at[octet], high_dev)
+
+    def own(t, k, name):
+        octet = dict(unit(rs_blocks, t, k))[name]
+        ring = rs_a if name == "a" else rs_b
+        await_recv(("e_high", t, k, name), e_high.at[octet])
+        await_recv(("e_low", t, k, name), e_low.at[octet])
+        if t:
+            await_recv(("ring", t - 1, k, name), ring.at[t - 1, k])
+        part[core, octet, first] = part[core, octet, first] + e_low[octet]
+        part[core, octet, last] = part[core, octet, last] + e_high[octet]
+        if t:
+            part[core, octet, middle] = part[core, octet, middle] + ring[t - 1, k]
+        if t < 3:
+            to(("ring", t, k, name), part.at[core, octet, middle], ring.at[t, k], up if name == "a" else down)
+        else:
+            cur[core, octet, middle] = cur[core, octet, middle] * part[core, octet, middle]
 
     def region(half, octet, start=0, count=EXT):
         return cur.at[half, octet, pl.ds(start, count)]
@@ -351,142 +382,135 @@
     a_far, b_far = 2 * far_row, 2 * far_row + 1
     gather_blocks = [(a_own, b_own), (a_prev, b_next), (b_prev, a_next), (a_far, b_far)]
 
-    def gather_and_blur(pending):
-        def to(name, src, dst, device):
-            pending.append(send(name, src, dst, device))
-
-        def pass_on(n, name, octet, device):
-            to(("y", n, name), middle_of(octet), middle_of(octet), device)
-
-        def halos(n):
-            for name, octet in unit(gather_blocks, n):
-                if n > 1:
-                    await_recv(("y", n, name), middle_of(octet))
-                if n in (2, 3):
-                    pass_on(n + 4, name, octet, up if name == "a" else down)
-                to(("h_high", n, name), region(core, octet, HALO, HALO), region(core, octet, HALO + DEPTH, HALO), low_dev)
-                to(("h_low", n, name), region(core, octet, DEPTH, HALO), region(core, octet, 0, HALO), high_dev)
-
-        def share(n):
-            for name, octet in unit(gather_blocks, n):
-                await_recv(("h_high", n, name), region(core, octet, HALO + DEPTH, HALO))
-                await_recv(("h_low", n, name), region(core, octet, 0, HALO))
-                to(("share", n, name), region(core, octet), region(core, octet), sibling)
-
-        def blur(n):
-            pairs = unit(gather_blocks, n)
-            for name, octet in pairs:
-                await_recv(("share", n, name), region(1 - core, octet))
-            blur_octets([octet for _, octet in pairs])
-
-        for k in range(2):
-            pass_on(2 + k, "a", a_own * 2 + k, up)
-            pass_on(2 + k, "b", b_own * 2 + k, down)
-        halos(0)
-        halos(1)
-        for k in range(2):
-            pass_on(4 + k, "a", b_own * 2 + k, up)
-            pass_on(4 + k, "b", a_own * 2 + k, down)
-        for n in range(2, 12):
-            if n < 8:
-                halos(n)
-            if 2 <= n < 10:
-                share(n - 2)
-            if n >= 4:
-                blur(n - 4)
-        return pending
-
-    def finish(pending):
-        for handle in pending:
-            handle.wait_send()
+    def pass_on(u, k, name):
+        device = up if name == "a" else down
+        if u == 3:
+            octet = dict(unit(gather_blocks, 1, k))[name]
+        else:
+            octet = ((a_own, b_own) if (u == 1) == (name == "a") else (b_own, a_own))[0] * 2 + k
+        to(("y", u, k, name), middle_of(octet), middle_of(octet), device)
+
+    def halos(u, k, name):
+        octet = dict(unit(gather_blocks, u, k))[name]
+        if u:
+            await_recv(("y", u, k, name), middle_of(octet))
+        if u == 1:
+            pass_on(3, k, name)
+        if u < 3 or (k, name) not in FORWARDED:
+            to(("h_high", u, k, name), region(core, octet, HALO, HALO), region(core, octet, HALO + DEPTH, HALO), low_dev)
+            to(("h_low", u, k, name), region(core, octet, DEPTH, HALO), region(core, octet, 0, HALO), high_dev)
+
+    halos_here = set()
+
+    def await_halos(u, k, name, octet):
+        if (u, k, name) in halos_here:
+            return
+        halos_here.add((u, k, name))
+        await_recv(("h_high", u, k, name), region(core, octet, HALO + DEPTH, HALO))
+        await_recv(("h_low", u, k, name), region(core, octet, 0, HALO))
+
+    def forward(u, k, name):
+        octet = dict(unit(gather_blocks, u, k))[name]
+        await_halos(u, k, name, octet)
+        device = up if name == "a" else down
+        for side_name, start in (("h_high", HALO + DEPTH), ("h_low", 0)):
+            to((side_name, 3, k, name), region(core, octet, start, HALO), region(core, octet, start, HALO), device)
+
+    def share(u, k, name):
+        octet = dict(unit(gather_blocks, u, k))[name]
+        await_halos(u, k, name, octet)
+        to(("share", u, k, name), region(core, octet), region(core, octet), sibling)
+
+    def blur(u, k, _):
+        pairs = unit(gather_blocks, u, k)
+        for name, octet in pairs:
+            await_recv(("share", u, k, name), region(1 - core, octet))
+        blur_octets([octet for _, octet in pairs])
+
+    def reduce_and_gather():
+        steps = {"C": compute, "E": edges, "O": own, "Y": pass_on, "H": halos, "F": forward, "S": share, "B": blur}
+        halos_here.clear()
+        for kind, stage, k, name in GATHER_ORDER:
+            steps[kind](stage, k, name)
 
     lanes = pl.ds(pl.multiple_of(core * HALF, HALF), HALF)
 
-    def final_gather(pending):
-        def both(block):
-            return pl.ds(block * 2, 2)
-
-        def held(block):
-            return gat.at[both(block)]
-
-        def middle_of(block):
-            return cur.at[core, both(block), pl.ds(HALO, DEPTH)]
-
-        def octet_own(octet):
-            return cur.at[core, octet, pl.ds(HALO, DEPTH)]
-
-        def to(name, src, dst, device):
-            pending.append(send(name, src, dst, device))
-
-        def write(block, own_slab):
+    def reduce_and_finish():
+        def held(octet):
+            return gat.at[octet]
+
+        def write(octet, own_slab):
             here = native if own_slab else foreign
-
-            def pieces():
-                for k in range(2):
-                    octet = block * 2 + k
-                    src = octet_own(octet) if own_slab else gat.at[octet]
-                    yield src, out.at[:, pl.ds(pl.multiple_of(octet * 8, 8), 8), lanes]
+            src = middle_of(octet) if own_slab else held(octet)
+            dst = out.at[:, octet_rows(octet), lanes]
 
             @pl.when(here)
             def _():
-                for src, dst in pieces():
-                    pltpu.make_async_copy(src, dst, out_sem.at[0]).start()
+                pltpu.make_async_copy(src, dst, out_sem.at[0]).start()
 
             @pl.when(jnp.logical_not(here))
             def _():
-                for src, dst in pieces():
-                    pltpu.make_async_remote_copy(
-                        src_ref=src, dst_ref=dst, send_sem=out_sem.at[1], recv_sem=out_sem.at[2],
-                        device_id=sibling, device_id_type=MESH).start()
-
-        to(("x", 0), middle_of(a_own), held(a_own), partner)
-        to(("by", 0), middle_of(b_own), middle_of(b_own), up)
-        to(("by", 1), middle_of(b_own), middle_of(b_own), down)
-        to(("x", 1), middle_of(b_own), held(b_own), partner)
-        to(("ay", 0), middle_of(a_own), middle_of(a_own), up)
-        to(("ay", 1), middle_of(a_own), middle_of(a_own), down)
-        write(a_own, True)
-        write(b_own, True)
-        await_recv(("x", 0), held(a_own))
-        to(("gy", 0), held(a_own), held(a_own), up)
-        to(("gy", 1), held(a_own), held(a_own), down)
-        write(a_own, False)
-        await_recv(("by", 0), middle_of(b_prev))
-        to(("bf", 0), octet_own(b_prev * 2), octet_own(b_prev * 2), up)
-        to(("x", 2), middle_of(b_prev), held(b_prev), partner)
-        await_recv(("by", 1), middle_of(b_next))
-        to(("bf", 1), octet_own(b_next * 2 + 1), octet_own(b_next * 2 + 1), down)
-        to(("x", 3), middle_of(b_next), held(b_next), partner)
-        write(b_prev, True)
-        write(b_next, True)
-        await_recv(("x", 1), held(b_own))
-        write(b_own, False)
-        await_recv(("ay", 1), middle_of(a_next))
-        to(("af", 1), middle_of(a_next), middle_of(a_next), down)
-        await_recv(("ay", 0), middle_of(a_prev))
-        write(a_next, True)
-        write(a_prev, True)
-        await_recv(("bf", 0), octet_own(b_far * 2))
-        await_recv(("bf", 1), octet_own(b_far * 2 + 1))
-        to(("x", 4), middle_of(b_far), held(b_far), partner)
-        write(b_far, True)
-        await_recv(("gy", 0), held(a_prev))
-        to(("gf", 0), held(a_prev), held(a_prev), up)
-        await_recv(("gy", 1), held(a_next))
-        write(a_prev, False)
-        write(a_next, False)
-        await_recv(("x", 2), held(b_prev))
-        write(b_prev, False)
-        await_recv(("x", 3), held(b_next))
-        write(b_next, False)
-        await_recv(("af", 1), middle_of(a_far))
-        write(a_far, True)
-        await_recv(("gf", 0), held(a_far))
-        write(a_far, False)
-        await_recv(("x", 4), held(b_far))
-        write(b_far, False)
-        for handle in pending:
-            handle.wait_send()
+                pltpu.make_async_remote_copy(
+                    src_ref=src, dst_ref=dst, send_sem=out_sem.at[1], recv_sem=out_sem.at[2],
+                    device_id=sibling, device_id_type=MESH).start()
+
+        moves = {
+            "xa": (middle_of, a_own, partner, None),
+            "xb": (middle_of, b_own, partner, None),
+            "ya+": (middle_of, a_own, up, None),
+            "ya-": (middle_of, a_own, down, None),
+            "yb+": (middle_of, b_own, up, None),
+            "yb-": (middle_of, b_own, down, None),
+            "g+": (held, a_own, up, "xa"),
+            "g-": (held, a_own, down, "xa"),
+            "xbp": (middle_of, b_prev, partner, "yb+"),
+            "xbn": (middle_of, b_next, partner, "yb-"),
+            "fa": (middle_of, a_next, down, "ya-"),
+            "gf": (held, a_prev, up, "g+"),
+            "gb": (held, b_prev, up, "xbp"),
+            "xbf": (middle_of, b_far, partner, "fb"),
+        }
+        lands = {
+            "xa": (held, a_own), "xb": (held, b_own), "xbp": (held, b_prev), "xbn": (held, b_next),
+            "xbf": (held, b_far), "ya+": (middle_of, a_prev), "ya-": (middle_of, a_next), "yb+": (middle_of, b_prev),
+            "yb-": (middle_of, b_next), "g+": (held, a_prev), "g-": (held, a_next), "fa": (middle_of, a_far),
+            "fb": (middle_of, b_far), "gf": (held, a_far), "gb": (held, b_far),
+        }
+        arrived = []
+
+        def arrive(name, k):
+            if (name, k) in arrived:
+                return
+            arrived.append((name, k))
+            ref, block = lands[name]
+            octet = block * 2 + k
+            await_recv((name, k), ref(octet))
+            write(octet, ref is middle_of)
+
+        def move(name, k):
+            if name == "fb":
+                ref, block, device, before = (
+                    (middle_of, b_prev, up, "yb+") if k == 0 else (middle_of, b_next, down, "yb-"))
+            else:
+                ref, block, device, before = moves[name]
+            if before:
+                arrive(before, k)
+            octet = block * 2 + k
+            src, dst = ref(octet), held(octet) if device is partner else ref(octet)
+            to((name, k), src, dst, device)
+
+        steps = {"C": compute, "E": edges, "O": own}
+        for kind, stage, k, name in FINISH_ORDER:
+            if kind in steps:
+                steps[kind](stage, k, name)
+                if (kind, stage) == ("O", 3):
+                    write((a_own if name == "a" else b_own) * 2 + k, True)
+            else:
+                move(kind, k)
+        for kind, stage, k, name in FINISH_ORDER:
+            if kind not in steps:
+                arrive(kind, k)
+        finish()
         half_out = out.at[:, :, pl.ds(0, HALF)]
         pltpu.make_async_copy(half_out, half_out, out_sem.at[0]).wait()
         final = pltpu.make_async_remote_copy(
@@ -547,13 +571,11 @@
         for g in range(GROUPS):
             copy(("rec", g), recording.at[0, pl.ds(g * GROUP, GROUP)], group(g), cross).wait_send()
 
-    sent = reduce_scatter()
     for step in range(1, ITERS):
-        sent = gather_and_blur(sent)
+        reduce_and_gather()
         quotient_planes(0, DEPTH)
-        finish(sent)
-        sent = reduce_scatter()
-    final_gather(sent)
+        finish()
+    reduce_and_finish()
 
 
 def shards(estimate, views_data, counts, psf):
@@ -563,9 +585,10 @@
     return pl.pallas_call(
         kernel,
         out_shape=jax.ShapeDtypeStruct((DEPTH, ROWS, COLS), F32),
-        in_specs=[hbm, hbm, vmem, vmem],
+        in_specs=[hbm, hbm, hbm, vmem],
         out_specs=any_space,
         scratch_shapes=[
+            pltpu.VMEM((8, DEPTH, ROWS), jnp.int32),
             pltpu.VMEM((2, OCTETS, PAD, 8, HALF), F32),
             pltpu.VMEM((DEPTH, ROWS, COLS), F32),
             pltpu.VMEM((DEPTH, ROWS, COLS), F32),
@@ -590,13 +613,13 @@
             pltpu.VMEM((2, PAD * 8, DEPTH * 8), BF16),
             pltpu.SemaphoreType.DMA((SEMS,)),
             pltpu.SemaphoreType.DMA((SEMS,)),
-            pltpu.SemaphoreType.DMA((2,)),
+            pltpu.SemaphoreType.DMA((3,)),
             pltpu.SemaphoreType.DMA((3,)),
         ],
         compiler_params=pltpu.CompilerParams(
             collective_id=0, has_side_effects=True, vmem_limit_bytes=47 * 2**20),
         cost_estimate=pl.CostEstimate(flops=2 * 10**10, bytes_accessed=2 * 10**7, transcendentals=0),
-    )(estimate, views_data, counts, psf)
+    )(estimate, views_data, counts, jnp.transpose(psf, (1, 0, 2)))
 
 
 def solution(mesh):

time: 182 us -> 175 us (0.962)
  Pallas kernels: 178 us -> 171 us
    pallas_call x1, Pallas kernels: 178 us -> 171 us  [shards(): pl.pallas_call(kernel, out_shape=jax.ShapeDtypeStruct((DEPTH, ROWS, COLS)...]
where the time goes in v4:
time: 175 us
  Pallas kernels  171 us (98%)
  local copies, waits for them, and re-layouts  3.6 us (2%)
    pallas_call x1, Pallas kernels, shards(): pl.pallas_call(kernel, out_shape=jax.ShapeDtypeStruct((DEPTH, ROWS, COLS)...  171 us
    unnamed x5, local copies, waits for them, and re-layouts  3.6 us

profile of v4, /device:TPU:1, one launch (start us, length us, event | category | flops | bytes accessed | tf_op | source)
XLA Modules:
  0.0 174.9 jit_solution(13834640595465204530)
XLA Ops:
  0.0 0.0 copy-start
  0.0 0.9 copy-done
  0.9 0.0 copy-start.1
  0.9 0.7 copy-done.1
  1.6 171.3 %shard_map.46 = f32[32,128,256]{2,1,0:T(8,128)S(1)} custom-call(f32[32,128,256]{2,1,0:T(8,128)} %est.1, f32[1,32,128,256]{3,2,1,0:T(8,128)} %recording.1, s32[8,32,128]{2,1,0:T(8,128)S(1)} %copy-done, f32[3,1,31]{2,1,0:T(1,128)S(1)} %bitcast.1), custom_call_target="tpu_custom_call" | custom-call | flops 20000000000 | bytes 20000000 | tf_op jit(solution)/shard_map/pallas_call | solution.py:585
  172.9 2.0 %copy.6 = f32[32,128,256]{2,1,0:T(8,128)} copy(f32[32,128,256]{2,1,0:T(8,128)S(1)} %shard_map.46) | data formatting | bytes 8388608
Async XLA Ops:
  0.0 0.9 copy-start
  0.9 0.7 copy-start.1

commit v5 on v4

--- a/solution.py
+++ b/solution.py
@@ -142,10 +142,18 @@
         copy(name, dst, dst, sibling).wait_recv()
 
     pltpu.make_async_copy(counts_in, counts, load_sem.at[2]).start()
+    has_low, has_high = chip > 0, chip < 15
+    has_outer = jnp.where(side == 0, chip, 15 - chip) > 0
+    outer_native = native & has_outer
+    has_cross = foreign | has_outer
     barrier = pltpu.get_barrier_semaphore()
-    for device in (sibling, low_dev, high_dev, down, up, cross):
+    for device in (sibling, down, up):
         pl.semaphore_signal(barrier, inc=1, device_id=device, device_id_type=MESH)
-    pl.semaphore_wait(barrier, 6)
+    for there, device in ((has_low, low_dev), (has_high, high_dev), (has_cross, cross)):
+        @pl.when(there)
+        def _():
+            pl.semaphore_signal(barrier, inc=1, device_id=device, device_id_type=MESH)
+    pl.semaphore_wait(barrier, 3 + jnp.where(has_low, 1, 0) + jnp.where(has_high, 1, 0) + jnp.where(has_cross, 1, 0))
 
     near = jnp.where(side == 0, EXT - HALO, 0)
     outer = jnp.where(side == 0, 0, EXT - HALO)
@@ -204,12 +212,16 @@
     def _():
         wext[HALO:HALO + DEPTH] = wraw[...]
         send("w_own", rows_of(HALO, DEPTH), rows_of(HALO, DEPTH), sibling)
-        send("w_outer", rows_of(own_edge, HALO), rows_of(near, HALO), cross)
         whole = planes(HALO, DEPTH)
         pltpu.make_async_copy(whole, whole, load_sem.at[0]).wait()
-        for k in range(4):
-            send(("est_outer", k), cur.at[:, 4 * k:4 * k + 4, pl.ds(own_edge, HALO)],
-                 cur.at[:, 4 * k:4 * k + 4, pl.ds(near, HALO)], cross)
+
+        @pl.when(has_outer)
+        def _():
+            send("w_outer", rows_of(own_edge, HALO), rows_of(near, HALO), cross)
+            for k in range(4):
+                send(("est_outer", k), cur.at[:, 4 * k:4 * k + 4, pl.ds(own_edge, HALO)],
+                     cur.at[:, 4 * k:4 * k + 4, pl.ds(near, HALO)], cross)
+
         send("est_own", whole, whole, sibling)
 
     @pl.when(foreign)
@@ -226,6 +238,22 @@
     def _(octet):
         for half in range(2):
             cur[half, octet, EXT:PAD] = jnp.zeros((PAD - EXT, 8, HALF), F32)
+
+    @pl.when(jnp.logical_not(has_outer))
+    def _():
+        wext[pl.ds(outer, HALO)] = jnp.zeros((HALO, 8, HALF), F32)
+
+        @pl.loop(0, OCTETS)
+        def _(octet):
+            for half in range(2):
+                cur[half, octet, pl.ds(outer, HALO)] = jnp.zeros((HALO, 8, HALF), F32)
+
+    for there, ref in ((has_low, e_low), (has_high, e_high)):
+        @pl.when(jnp.logical_not(there))
+        def _():
+            @pl.loop(0, OCTETS)
+            def _(octet):
+                ref[octet] = jnp.zeros((HALO, 8, HALF), F32)
 
     @pl.when(foreign)
     def _():
@@ -275,14 +303,20 @@
 
     @pl.when(native)
     def _():
-        await_recv("w_outer", rows_of(outer, HALO))
-        send("w_outer_on", rows_of(outer, HALO), rows_of(outer, HALO), sibling)
+        @pl.when(has_outer)
+        def _():
+            await_recv("w_outer", rows_of(outer, HALO))
+            send("w_outer_on", rows_of(outer, HALO), rows_of(outer, HALO), sibling)
+
         await_recv("w_near", rows_of(near, HALO))
 
     @pl.when(foreign)
     def _():
         await_recv("w_own", rows_of(HALO, DEPTH))
-        await_recv("w_outer_on", rows_of(outer, HALO))
+
+        @pl.when(has_outer)
+        def _():
+            await_recv("w_outer_on", rows_of(outer, HALO))
 
     own_weight = jnp.where(core == 0, wext[:, 0, :], wext[:, 1, :])
     wt[:, 0:PAD] = own_weight.T
@@ -305,9 +339,11 @@
             mid[:, octet_rows(octet), :] = value.reshape(DEPTH, 8, COLS)
 
     def quotient_planes(first, count):
-        @pl.loop(0, count // 4)
+        together = min(count, 8)
+
+        @pl.loop(0, count // together)
         def _(k):
-            at = [first + 4 * k + i for i in range(4)]
+            at = [first + together * k + i for i in range(together)]
             values = [from_left(y_blur, mid[z]) for z in at]
             values = [rec[z] / value for z, value in zip(at, values)]
             values = [from_left(y_back, value) for value in values]
@@ -331,15 +367,48 @@
         return [(name, block * 2 + k) for name, block in zip("ab", blocks[t])]
 
     first, last, middle = pl.ds(HALO, HALO), pl.ds(DEPTH, HALO), pl.ds(HALO, DEPTH)
-    pending = []
+    pending, sided = [], []
 
     def to(name, src, dst, device):
-        pending.append(send(name, src, dst, device))
+        send(name, src, dst, device)
+        pending.append((name, src, dst, device))
+
+    def to_both(high_name, high, low_name, low):
+        @pl.when(has_low)
+        def _():
+            send(high_name, *high, low_dev)
+
+        @pl.when(has_high)
+        def _():
+            send(low_name, *low, high_dev)
+
+        sided.append((high_name, *high, low_name, *low))
+
+    def from_both(high_name, high, low_name, low):
+        @pl.when(has_high)
+        def _():
+            await_recv(high_name, high)
+
+        @pl.when(has_low)
+        def _():
+            await_recv(low_name, low)
 
     def finish():
-        for handle in pending:
-            handle.wait_send()
+        for name, src, dst, device in pending:
+            copy(name, src, dst, device).wait_send()
+
+        @pl.when(has_low)
+        def _():
+            for name, src, dst, _, _, _ in sided:
+                copy(name, src, dst, low_dev).wait_send()
+
+        @pl.when(has_high)
+        def _():
+            for _, _, _, name, src, dst in sided:
+                copy(name, src, dst, high_dev).wait_send()
+
         pending.clear()
+        sided.clear()
 
     def compute(t, k, _):
         pairs = unit(rs_blocks, t, k)
@@ -351,14 +420,13 @@
         octet = dict(unit(rs_blocks, t, k))[name]
         await_recv(("sib", t, k, name), rsib.at[octet])
         part[core, octet] = part[core, octet] + rsib[octet]
-        to(("e_high", t, k, name), part.at[core, octet, pl.ds(0, HALO)], e_high.at[octet], low_dev)
-        to(("e_low", t, k, name), part.at[core, octet, pl.ds(HALO + DEPTH, HALO)], e_low.at[octet], high_dev)
+        to_both(("e_high", t, k, name), (part.at[core, octet, pl.ds(0, HALO)], e_high.at[octet]),
+                ("e_low", t, k, name), (part.at[core, octet, pl.ds(HALO + DEPTH, HALO)], e_low.at[octet]))
 
     def own(t, k, name):
         octet = dict(unit(rs_blocks, t, k))[name]
         ring = rs_a if name == "a" else rs_b
-        await_recv(("e_high", t, k, name), e_high.at[octet])
-        await_recv(("e_low", t, k, name), e_low.at[octet])
+        from_both(("e_high", t, k, name), e_high.at[octet], ("e_low", t, k, name), e_low.at[octet])
         if t:
             await_recv(("ring", t - 1, k, name), ring.at[t - 1, k])
         part[core, octet, first] = part[core, octet, first] + e_low[octet]
@@ -397,8 +465,9 @@
         if u == 1:
             pass_on(3, k, name)
         if u < 3 or (k, name) not in FORWARDED:
-            to(("h_high", u, k, name), region(core, octet, HALO, HALO), region(core, octet, HALO + DEPTH, HALO), low_dev)
-            to(("h_low", u, k, name), region(core, octet, DEPTH, HALO), region(core, octet, 0, HALO), high_dev)
+            to_both(("h_high", u, k, name),
+                    (region(core, octet, HALO, HALO), region(core, octet, HALO + DEPTH, HALO)),
+                    ("h_low", u, k, name), (region(core, octet, DEPTH, HALO), region(core, octet, 0, HALO)))
 
     halos_here = set()
 
@@ -406,15 +475,19 @@
         if (u, k, name) in halos_here:
             return
         halos_here.add((u, k, name))
-        await_recv(("h_high", u, k, name), region(core, octet, HALO + DEPTH, HALO))
-        await_recv(("h_low", u, k, name), region(core, octet, 0, HALO))
+        high, low = region(core, octet, HALO + DEPTH, HALO), region(core, octet, 0, HALO)
+        if u == 3 and (k, name) in FORWARDED:
+            await_recv(("f_high", k, name), high)
+            await_recv(("f_low", k, name), low)
+        else:
+            from_both(("h_high", u, k, name), high, ("h_low", u, k, name), low)
 
     def forward(u, k, name):
         octet = dict(unit(gather_blocks, u, k))[name]
         await_halos(u, k, name, octet)
         device = up if name == "a" else down
-        for side_name, start in (("h_high", HALO + DEPTH), ("h_low", 0)):
-            to((side_name, 3, k, name), region(core, octet, start, HALO), region(core, octet, start, HALO), device)
+        for side_name, start in (("f_high", HALO + DEPTH), ("f_low", 0)):
+            to((side_name, k, name), region(core, octet, start, HALO), region(core, octet, start, HALO), device)
 
     def share(u, k, name):
         octet = dict(unit(gather_blocks, u, k))[name]
@@ -530,12 +603,12 @@
     for k in range(4):
         strip = cur.at[:, 4 * k:4 * k + 4, pl.ds(outer, HALO)]
 
-        @pl.when(native)
+        @pl.when(outer_native)
         def _():
             await_recv(("est_outer", k), strip)
             send(("est_on", k), strip, strip, sibling)
 
-        @pl.when(foreign)
+        @pl.when(foreign & has_outer)
         def _():
             await_recv(("est_on", k), strip)
 
@@ -555,9 +628,12 @@
     @pl.when(native)
     def _():
         copy("w_own", rows_of(HALO, DEPTH), rows_of(HALO, DEPTH), sibling).wait_send()
+        copy("est_own", planes(HALO, DEPTH), planes(HALO, DEPTH), sibling).wait_send()
+
+    @pl.when(outer_native)
+    def _():
         copy("w_outer", rows_of(own_edge, HALO), rows_of(near, HALO), cross).wait_send()
         copy("w_outer_on", rows_of(outer, HALO), rows_of(outer, HALO), sibling).wait_send()
-        copy("est_own", planes(HALO, DEPTH), planes(HALO, DEPTH), sibling).wait_send()
         for k in range(4):
             strip = cur.at[:, 4 * k:4 * k + 4, pl.ds(outer, HALO)]
             copy(("est_outer", k), strip, strip, cross).wait_send()

time: 175 us -> 169 us (0.966)
  Pallas kernels: 171 us -> 165 us
    pallas_call x1, Pallas kernels: 171 us -> 165 us  [shards(): pl.pallas_call(kernel, out_shape=jax.ShapeDtypeStruct((DEPTH, ROWS, COLS)...]
where the time goes in v5:
time: 169 us; the launch traced here: 168 us
  Pallas kernels  165 us (98%)
  local copies, waits for them, and re-layouts  3.6 us (2%)
    pallas_call x1, Pallas kernels, shards(): pl.pallas_call(kernel, out_shape=jax.ShapeDtypeStruct((DEPTH, ROWS, COLS)...  165 us
    unnamed x5, local copies, waits for them, and re-layouts  3.6 us

profile of v5, /device:TPU:1, one launch (start us, length us, event | category | flops | bytes accessed | tf_op | source)
XLA Modules:
  0.0 168.4 jit_solution(3671662254540072800)
XLA Ops:
  0.0 0.0 copy-start
  0.0 0.9 copy-done
  0.9 0.0 copy-start.1
  0.9 0.7 copy-done.1
  1.6 164.8 %shard_map.46 = f32[32,128,256]{2,1,0:T(8,128)S(1)} custom-call(f32[32,128,256]{2,1,0:T(8,128)} %est.1, f32[1,32,128,256]{3,2,1,0:T(8,128)} %recording.1, s32[8,32,128]{2,1,0:T(8,128)S(1)} %copy-done, f32[3,1,31]{2,1,0:T(1,128)S(1)} %bitcast.1), custom_call_target="tpu_custom_call" | custom-call | flops 20000000000 | bytes 20000000 | tf_op jit(solution)/shard_map/pallas_call | solution.py:661
  166.4 2.0 %copy.6 = f32[32,128,256]{2,1,0:T(8,128)} copy(f32[32,128,256]{2,1,0:T(8,128)S(1)} %shard_map.46) | data formatting | bytes 8388608
Async XLA Ops:
  0.0 0.9 copy-start
  0.9 0.7 copy-start.1

commit v6 on v5

--- a/solution.py
+++ b/solution.py
@@ -393,22 +393,23 @@
         def _():
             await_recv(low_name, low)
 
-    def finish():
-        for name, src, dst, device in pending:
+    def finish(keep=0, keep_sided=0):
+        over = pending[:len(pending) - keep]
+        over_sided = sided[:len(sided) - keep_sided]
+        for name, src, dst, device in over:
             copy(name, src, dst, device).wait_send()
 
         @pl.when(has_low)
         def _():
-            for name, src, dst, _, _, _ in sided:
+            for name, src, dst, _, _, _ in over_sided:
                 copy(name, src, dst, low_dev).wait_send()
 
         @pl.when(has_high)
         def _():
-            for _, _, _, name, src, dst in sided:
+            for _, _, _, name, src, dst in over_sided:
                 copy(name, src, dst, high_dev).wait_send()
 
-        pending.clear()
-        sided.clear()
+        del pending[:len(over)], sided[:len(over_sided)]
 
     def compute(t, k, _):
         pairs = unit(rs_blocks, t, k)
@@ -503,7 +504,9 @@
     def reduce_and_gather():
         steps = {"C": compute, "E": edges, "O": own, "Y": pass_on, "H": halos, "F": forward, "S": share, "B": blur}
         halos_here.clear()
-        for kind, stage, k, name in GATHER_ORDER:
+        for at, (kind, stage, k, name) in enumerate(GATHER_ORDER):
+            if at == len(GATHER_ORDER) - 11:
+                finish(12, 4)
             steps[kind](stage, k, name)
 
     lanes = pl.ds(pl.multiple_of(core * HALF, HALF), HALF)
@@ -580,6 +583,7 @@
                     write((a_own if name == "a" else b_own) * 2 + k, True)
             else:
                 move(kind, k)
+        finish(24)
         for kind, stage, k, name in FINISH_ORDER:
             if kind not in steps:
                 arrive(kind, k)

time: 169 us -> 169 us (level)
  no operation moved by 1% of the time
where the time goes in v6:
time: 169 us; the launch traced here: 168 us
  Pallas kernels  165 us (98%)
  local copies, waits for them, and re-layouts  3.6 us (2%)
    pallas_call x1, Pallas kernels, shards(): pl.pallas_call(kernel, out_shape=jax.ShapeDtypeStruct((DEPTH, ROWS, COLS)...  165 us
    unnamed x5, local copies, waits for them, and re-layouts  3.6 us

profile of v6, /device:TPU:1, one launch (start us, length us, event | category | flops | bytes accessed | tf_op | source)
XLA Modules:
  0.0 168.4 jit_solution(13995820920501820017)
XLA Ops:
  0.0 0.0 copy-start
  0.0 0.9 copy-done
  0.9 0.0 copy-start.1
  0.9 0.7 copy-done.1
  1.6 164.8 %shard_map.46 = f32[32,128,256]{2,1,0:T(8,128)S(1)} custom-call(f32[32,128,256]{2,1,0:T(8,128)} %est.1, f32[1,32,128,256]{3,2,1,0:T(8,128)} %recording.1, s32[8,32,128]{2,1,0:T(8,128)S(1)} %copy-done, f32[3,1,31]{2,1,0:T(1,128)S(1)} %bitcast.1), custom_call_target="tpu_custom_call" | custom-call | flops 20000000000 | bytes 20000000 | tf_op jit(solution)/shard_map/pallas_call | solution.py:665
  166.4 2.0 %copy.6 = f32[32,128,256]{2,1,0:T(8,128)} copy(f32[32,128,256]{2,1,0:T(8,128)S(1)} %shard_map.46) | data formatting | bytes 8388608
Async XLA Ops:
  0.0 0.9 copy-start
  0.9 0.7 copy-start.1
